TPU v7x, 1024 devices: a whole 8x8x8 slice. The times are simulated.
1024 devices in a mesh: row: 32 (over z, x_hi), col: 32 (over x_lo, y, core).
Axes of the slice: x: 8 (x_hi: 4, x_lo: 2; x = x_hi * 2 + x_lo), y: 8, z: 8, core: 2. Of those that a mesh axis runs over, the one named last changes fastest.
Arguments:
- features: bfloat16 [131072, 128], P(('row', 'col')), may hold values from -6 to 6
- weight: bfloat16 [128, 256], replicated, may hold values from -0.5 to 0.5
- tile_vals: bfloat16 [32, 32, 48, 128, 128], P('row', 'col'), may hold values from -0.125 to 0.125
- tile_rows: int32 [32, 32, 48], P('row', 'col'), may hold values from 0 to 31
- tile_cols: int32 [32, 32, 48], P('row', 'col'), may hold values from 0 to 31
- tile_counts: int32 [32, 32], P('row', 'col'), may hold values from 6 to 48, as said below
- cotangent: bfloat16 [131072, 256], P(('row', 'col')), may hold values from -6 to 6
Outputs:
- hidden: bfloat16 [131072, 256], P(('row', 'col'))
- grad_x: bfloat16 [131072, 128], P(('row', 'col'))
- grad_w: float32 [128, 256], replicated
Inputs may be any that keep to these rules, and one draw needn't show every extreme that they name: `tile_counts`: slots from this number on are ignored; some partition uses all 48 slots. `tile_rows`: a block pair may occur in several slots of a partition; their tiles add.
All inputs are finite; a program needn't handle non-finite values.
Results may differ from a plain program's by a relative error of at most 0.025.
Values may be sent and summed in bfloat16 or wider, within the bound.
No kernel may reach another device: no remote copies, remote signals or barrier semaphores. Data moves between devices by JAX's collectives and lax.ppermute only.
A program may use at most 32 MiB of HBM per device.

v0:
```python
import jax
import jax.numpy as jnp
from jax import lax
from jax.sharding import PartitionSpec as P


def tile_sums(tile_set, rows_out, rows_in, tile_count, source, n_out, pattern):
    edge_size = tile_set.shape[-1]
    feat_width = source.shape[-1]
    source_blocks = source.reshape(-1, edge_size, feat_width)

    def one_group(group_index, summed):
        first_slot = group_index * 16
        tile_group = lax.dynamic_slice_in_dim(tile_set, first_slot, 16, 0)
        out_group = lax.dynamic_slice_in_dim(rows_out, first_slot, 16, 0)
        in_group = lax.dynamic_slice_in_dim(rows_in, first_slot, 16, 0)
        gathered = jnp.take(source_blocks, in_group, axis=0)
        product = jnp.einsum(pattern, tile_group, gathered, preferred_element_type=jnp.float32)
        active = (first_slot + jnp.arange(16, dtype=jnp.int32) < tile_count).astype(jnp.float32)
        return summed.at[out_group].add(product * active[:, None, None])

    initial = jnp.zeros((n_out, edge_size, feat_width), jnp.float32)
    last_group = tile_set.shape[0] // 16
    summed = lax.fori_loop(0, last_group, one_group, initial)
    return summed.reshape(n_out * edge_size, feat_width)


def shards(features, weight, tile_vals, tile_rows, tile_cols, tile_counts, cotangent):
    tiles_here = tile_vals[0, 0]
    rows_here = tile_rows[0, 0]
    cols_here = tile_cols[0, 0]
    tile_count = tile_counts[0, 0]
    owned = features.shape[0]
    edge_size = tiles_here.shape[-1]
    column_stripe = lax.all_gather(features, "row", axis=0, tiled=True)
    row_blocks = lax.axis_size("col") * owned // edge_size
    partial_rows = tile_sums(
        tiles_here, rows_here, cols_here, tile_count, column_stripe, row_blocks, "tij,tjh->tih"
    )
    summed_rows = lax.psum_scatter(
        partial_rows.astype(jnp.bfloat16), "col", scatter_dimension=0, tiled=True
    )
    preact = jnp.dot(summed_rows, weight, preferred_element_type=jnp.float32)
    negative = jnp.expm1(jnp.minimum(preact, 0.0))
    hidden = jnp.where(preact > 0, preact, negative).astype(jnp.bfloat16)
    slope = jnp.where(preact > 0, 1.0, negative + 1.0)
    upstream = (cotangent.astype(jnp.float32) * slope).astype(jnp.bfloat16)
    local_grad = lax.dot_general(
        summed_rows, upstream, (((0,), (0,)), ((), ())), preferred_element_type=jnp.float32
    )
    grad_w = lax.psum(local_grad, ("row", "col"))
    row_stripe = lax.dot_general(
        lax.all_gather(upstream, "col", axis=0, tiled=True),
        weight,
        (((1,), (1,)), ((), ())),
        preferred_element_type=jnp.float32,
    ).astype(jnp.bfloat16)
    col_blocks = lax.axis_size("row") * owned // edge_size
    partial_cols = tile_sums(
        tiles_here, cols_here, rows_here, tile_count, row_stripe, col_blocks, "tji,tjh->tih"
    )
    summed_cols = lax.psum_scatter(
        partial_cols.astype(jnp.bfloat16), "row", scatter_dimension=0, tiled=True
    )
    return (hidden, summed_cols, grad_w)


def solution(mesh):
    placed = (
        P(("row", "col"), None),
        P(),
        P("row", "col", None, None, None),
        P("row", "col", None),
        P("row", "col", None),
        P("row", "col"),
        P(("row", "col"), None),
    )
    return jax.shard_map(
        shards,
        mesh=mesh,
        in_specs=placed,
        out_specs=(P(("row", "col"), None), P(("row", "col"), None), P()),
        check_vma=False,
    )
```

profile of v0, /device:TPU:4, one launch (start us, length us, event | category | flops | bytes accessed | tf_op | source)
XLA Modules:
  0.0 845.1 jit_solution(12852764446217117074)
XLA Ops:
  7.2 0.0 copy-start
  7.2 0.0 copy-start.4
  7.2 0.0 copy-start.1
  7.2 0.0 copy-start.5
  7.2 0.0 all-gather.3.cloned.1.call-start
  7.3 0.7 all-gather.3.cloned.1.call-update
  7.9 0.0 reduce-scatter.3.cloned.1.call-start
  8.0 105.7 %all-gather.3.cloned.1.call-done = bf16[4096,128]{1,0:T(8,128)(2,1)} async-done(((bf16[128,128]{1,0:T(8,128)(2,1)}), bf16[4096,128]{1,0:T(8,128)(2,1)}) %all-gather.3.cloned.1.call-update) | async-done | bytes 1048592 | tf_op jit(solution)/shard_map/all_gather | solution.py:35
  113.7 1.6 broadcast.71.clone
  115.2 0.0 copy-done.4
  115.2 0.0 copy-done.1
  115.2 0.0 copy-done.5
  115.2 19.3 %while.26 = (s32[]{:T(128)}, f32[32,128,128]{2,1,0:T(8,128)}, s32[48]{0:T(128)S(1)}, bf16[48,128,128]{2,1,0:T(8,128)(2,1)S(1)}, s32[48]{0:T(128)S(1)}, /*index=5...) while((s32[]{:T(128)}, f32[32,128,128]{2,1,0:T(8,128)}, ...), condition=%wide.region_2.0_spmd, body=%wide.region_0.3_spmd.sunk | while | flops 67896520 | bytes 6297287 | solution.py:24
  115.3 0.1 compare_select_fusion.10
  115.3 0.7 compare_and_fusion.4
  116.1 1.9 gather_fusion
  118.0 0.4 convolution_multiply_fusion.4
  118.3 3.4 scatter_fusion
  121.7 0.1 compare_select_fusion.10
  121.8 0.7 compare_and_fusion.4
  122.5 1.9 gather_fusion
  124.4 0.4 convolution_multiply_fusion.4
  124.8 3.4 scatter_fusion
  128.1 0.1 compare_select_fusion.10
  128.2 0.7 compare_and_fusion.4
  128.9 1.9 gather_fusion
  130.8 0.4 convolution_multiply_fusion.4
  131.2 3.3 scatter_fusion
  134.6 2.8 convert_element_type.46
  137.3 0.0 reduce-scatter.3.cloned.1.call-update
  137.3 0.0 all-gather.5.cloned.1.call-start
  137.4 117.8 %reduce-scatter.3.cloned.1.call-done = bf16[128,128]{1,0:T(8,128)(2,1)} async-done(((bf16[4096,128]{1,0:T(8,128)(2,1)}), bf16[128,128]{1,0:T(8,128)(2,1)}) %reduce-scatter.3.cloned.1.call-update) | async-done | bytes 32784 | tf_op jit(solution)/shard_map/reduce_scatter | solution.py:40
  255.2 0.0 copy-done.6
  255.2 1.7 fusion.14
  256.9 0.0 all-gather.5.cloned.1.call-update
  256.9 0.0 all-reduce.2.cloned.1.call-start
  257.0 1.6 copy.10
  258.6 0.9 fusion.15
  259.4 0.0 all-reduce.2.cloned.1.call-update
  259.5 0.0 reduce-scatter.5.cloned.1.call-start
  259.5 64.7 %all-gather.5.cloned.1.call-done = bf16[4096,256]{1,0:T(8,128)(2,1)} async-done(((bf16[128,256]{1,0:T(8,128)(2,1)}), bf16[4096,256]{1,0:T(8,128)(2,1)}) %all-gather.5.cloned.1.call-update) | async-done | bytes 2097168 | tf_op jit(solution)/shard_map/all_gather | solution.py:53
  324.2 2.3 convolution_convert_fusion
  326.5 1.6 broadcast.71
  328.1 18.7 %while.27 = (s32[]{:T(128)}, f32[32,128,128]{2,1,0:T(8,128)}, s32[48]{0:T(128)S(1)}, bf16[48,128,128]{1,2,0:T(8,128)(2,1)}, s32[48]{0:T(128)S(1)}, /*index=5*/bf...) while((s32[]{:T(128)}, f32[32,128,128]{2,1,0:T(8,128)}, ...), condition=%wide.region_6.8_spmd, body=%wide.region_4.0_spmd.sunk | while | flops 67896520 | bytes 6296343 | solution.py:24
  328.1 0.1 compare_select_fusion.11
  328.2 0.7 compare_and_fusion.5
  328.9 0.6 gather_fusion.1
  329.5 1.4 convolution_multiply_fusion.5
  331.0 3.4 scatter_fusion.1
  334.3 0.1 compare_select_fusion.11
  334.4 0.7 compare_and_fusion.5
  335.1 0.6 gather_fusion.1
  335.8 1.4 convolution_multiply_fusion.5
  337.2 3.3 scatter_fusion.1
  340.5 0.1 compare_select_fusion.11
  340.6 0.7 compare_and_fusion.5
  341.4 0.6 gather_fusion.1
  342.0 1.4 convolution_multiply_fusion.5
  343.4 3.3 scatter_fusion.1
  346.8 2.7 convert_element_type.52
  349.5 0.0 reduce-scatter.5.cloned.1.call-update
  349.5 258.4 %all-reduce.2.cloned.1.call-done = f32[128,256]{1,0:T(8,128)} async-done(((f32[128,256]{1,0:T(8,128)}), f32[128,256]{1,0:T(8,128)}) %all-reduce.2.cloned.1.call-update) | async-done | bytes 131088 | tf_op jit(solution)/shard_map/psum | solution.py:51
  607.9 229.1 %reduce-scatter.5.cloned.1.call-done = bf16[128,128]{1,0:T(8,128)(2,1)} async-done(((bf16[4096,128]{1,0:T(8,128)(2,1)}), bf16[128,128]{1,0:T(8,128)(2,1)}) %reduce-scatter.5.cloned.1.call-update) | async-done | bytes 32784 | tf_op jit(solution)/shard_map/reduce_scatter | solution.py:62
  837.0 1.6 copy.28
  (12 shorter events, 0.0 us)
Async XLA Ops:
  7.2 248.1 %copy-start = (bf16[128,256]{1,0:T(8,128)(2,1)S(1)}, bf16[128,256]{1,0:T(8,128)(2,1)}, u32[]{:S(2)}) copy-start(bf16[128,256]{1,0:T(8,128)(2,1)} %param.14) | copy-start | bytes 196612
  7.2 108.1 %copy-start.4 = (s32[1,1,48]{2,1,0:T(1,128)S(1)}, s32[1,1,48]{2,1,0:T(1,128)}, u32[]{:S(2)}) copy-start(s32[1,1,48]{2,1,0:T(1,128)} %param.16) | copy-start | bytes 580
  7.2 108.1 %copy-start.1 = (bf16[1,1,48,128,128]{4,3,2,1,0:T(8,128)(2,1)S(1)}, bf16[1,1,48,128,128]{4,3,2,1,0:T(8,128)(2,1)}, u32[]{:S(2)}) copy-start(bf16[1,1,48,128,128]{4,3,2,1,0:T(8,128)(2,1)} %param.15) | copy-start | bytes 4718596
  7.2 108.0 %copy-start.5 = (s32[1,1,48]{2,1,0:T(1,128)S(1)}, s32[1,1,48]{2,1,0:T(1,128)}, u32[]{:S(2)}) copy-start(s32[1,1,48]{2,1,0:T(1,128)} %param.17) | copy-start | bytes 580
  7.2 106.5 %all-gather.3.cloned.1.call-start = ((), (), s32[]{:S(2)}) async-start(), calls=%async_computation.2 | async-start | bytes 1081344 | tf_op jit(solution)/shard_map/all_gather | solution.py:35
  7.9 247.3 %reduce-scatter.3.cloned.1.call-start = ((), (), s32[]{:S(2)}) async-start(), calls=%async_computation.3 | async-start | bytes 1081344 | tf_op jit(solution)/shard_map/reduce_scatter | solution.py:40
  134.6 120.7 %copy-start.6 = (bf16[128,256]{1,0:T(8,128)(2,1)S(1)}, bf16[128,256]{1,0:T(8,128)(2,1)}, u32[]{:S(2)}) copy-start(bf16[128,256]{1,0:T(8,128)(2,1)} %param.19) | copy-start | bytes 196612
  137.3 186.9 %all-gather.5.cloned.1.call-start = ((), (), s32[]{:S(2)}) async-start(), calls=%async_computation.4 | async-start | bytes 2162688 | tf_op jit(solution)/shard_map/all_gather | solution.py:53
  255.2 3.4 copy-start.3
  256.9 1.7 copy-start.2
  256.9 351.0 %all-reduce.2.cloned.1.call-start = ((), (), s32[]{:S(2)}) async-start(), calls=%async_computation.6 | async-start | bytes 262144 | tf_op jit(solution)/shard_map/psum | solution.py:51
  259.5 577.6 %reduce-scatter.5.cloned.1.call-start = ((), (), s32[]{:S(2)}) async-start(), calls=%async_computation.5 | async-start | bytes 1081344 | tf_op jit(solution)/shard_map/reduce_scatter | solution.py:62
Sparse Core Ops, SparseCore 0:
  12.4 101.2 all-gather.2
  137.5 117.7 reduce-scatter.2
  258.3 65.8 all-gather.4
  330.1 277.7 all-reduce.1
  613.9 223.0 reduce-scatter.4
where the time goes:
time: 846 us; the launch traced here: 845 us
  waiting for transfers between devices  776 us (92%)
  other arithmetic  30.4 us (4%)
  local copies, waits for them, and re-layouts  13.9 us (2%)
  between operations  13.8 us (2%)
  matrix products  10.2 us (1%)
    psum x1, waiting for transfers between devices, shards(): grad_w = lax.psum(local_grad, ('row', 'col'))  258 us
    reduce_scatter x1, waiting for transfers between devices, shards(): lax.psum_scatter(partial_cols.astype(jnp.bfloat16), 'row', scatter_dimens...  229 us
    reduce_scatter x1, waiting for transfers between devices, shards(): lax.psum_scatter(partial_rows.astype(jnp.bfloat16), 'col', scatter_dimens...  118 us
    all_gather x1, waiting for transfers between devices, shards(): column_stripe = lax.all_gather(features, 'row', axis=0, tiled=True)  106 us
    all_gather x1, waiting for transfers between devices, shards(): lax.all_gather(upstream, 'col', axis=0, tiled=True)  64.7 us
    scatter-add x6, other arithmetic, one_group(): return summed.at[out_group].add(product * active[:, None, None])  20.1 us
  transfers between devices with their start and end apart: 5, of which 5 were waited for; matrix products, arithmetic and copies ran while one was open for 3% of the time, Pallas kernels for 0%

commit v1 on v0

v1 whole, which is shorter than its diff:
```python
import functools

import jax
import jax.numpy as jnp
from jax import lax
from jax.experimental import pallas as pl
from jax.experimental.pallas import tpu as pltpu
from jax.sharding import Mesh, PartitionSpec as P

ROW = ("z", "x_hi")
PLANE = ("x_lo", "y")
CORE = "core"
COL = PLANE + (CORE,)
UNROLL = 4
VMEM_LIMIT = 32 * 1024 * 1024

SMEM_SPEC = pl.BlockSpec(memory_space=pltpu.SMEM)
VMEM_SPEC = pl.BlockSpec(memory_space=pltpu.VMEM)


def place(block, core):
    return ((block & 1) ^ core) * 16 + (block >> 1)


def add_tiles(count, slots, out_place, product, acc):
    spare = acc.shape[0] - 1

    def group(index, carry):
        first = index * UNROLL
        products = [product(first + j) for j in range(UNROLL)]
        for j in range(UNROLL):
            slot = first + j
            target = jnp.where(slot < count, out_place(slot), spare)
            acc[target] += products[j]
        return carry

    lax.fori_loop(0, (count + UNROLL - 1) // UNROLL, group, 0)


def forward_kernel(count_ref, rows_ref, cols_ref, tiles_ref, stripe_ref, keep_ref, send_ref, acc):
    core = lax.axis_index(CORE)
    acc[...] = jnp.zeros_like(acc)

    def product(k):
        return jnp.dot(tiles_ref[k], stripe_ref[cols_ref[0, k]], preferred_element_type=jnp.float32)

    add_tiles(count_ref[0, 0], tiles_ref.shape[0], lambda k: place(rows_ref[0, k], core), product, acc)
    half = keep_ref.shape[0]
    keep_ref[...] = acc[:half].astype(keep_ref.dtype)
    send_ref[...] = acc[half : 2 * half].astype(send_ref.dtype)


def dense_kernel(terms_ref, weight_ref, cot_ref, hidden_ref, payload_ref):
    groups, owned, _ = terms_ref.shape
    total = terms_ref[0].astype(jnp.float32)
    for i in range(1, groups):
        total += terms_ref[i].astype(jnp.float32)
    aggregated = total.astype(jnp.bfloat16)
    weight = weight_ref[...]
    preact = jnp.dot(aggregated, weight, preferred_element_type=jnp.float32)
    capped = jnp.minimum(preact, 0.0)
    grown = jnp.exp(capped)
    negative = grown - 1.0
    hidden_ref[...] = jnp.where(preact > 0, preact, negative).astype(jnp.bfloat16)
    slope = jnp.where(preact > 0, 1.0, grown)
    upstream = (cot_ref[...].astype(jnp.float32) * slope).astype(jnp.bfloat16)
    grad = lax.dot_general(
        aggregated, upstream, (((0,), (0,)), ((), ())), preferred_element_type=jnp.float32
    )
    back = lax.dot_general(
        weight, upstream, (((1,), (1,)), ((), ())), preferred_element_type=jnp.float32
    ).astype(jnp.bfloat16)
    step = grad.shape[0] // groups
    for i in range(groups):
        piece = grad[i * step : (i + 1) * step]
        packed = jnp.concatenate([piece[:, :128], piece[:, 128:]], axis=0)
        payload_ref[i, :owned] = back
        payload_ref[i, owned:] = packed.astype(jnp.bfloat16)


def backward_kernel(count_ref, rows_ref, cols_ref, tiles_ref, own_ref, other_ref, out_ref, acc, stripe):
    core = lax.axis_index(CORE)
    half = own_ref.shape[0]
    owned = stripe.shape[1]
    stripe[:half] = own_ref[:, :owned]
    stripe[half:] = other_ref[:, :owned]
    acc[...] = jnp.zeros_like(acc)

    def product(k):
        return jnp.dot(stripe[place(rows_ref[0, k], core)], tiles_ref[k], preferred_element_type=jnp.float32)

    add_tiles(count_ref[0, 0], tiles_ref.shape[0], lambda k: cols_ref[0, k], product, acc)
    grad = own_ref[0, owned:].astype(jnp.float32) + other_ref[0, owned:].astype(jnp.float32)
    for i in range(1, half):
        grad += own_ref[i, owned:].astype(jnp.float32) + other_ref[i, owned:].astype(jnp.float32)
    grad = grad.astype(out_ref.dtype)
    for i in range(out_ref.shape[0]):
        out_ref[i, :owned] = acc[i].astype(out_ref.dtype)
        out_ref[i, owned:] = grad


def final_kernel(terms_ref, grad_x_ref, piece_ref):
    groups, rows, owned = terms_ref.shape
    total = terms_ref[0].astype(jnp.float32)
    for i in range(1, groups):
        total += terms_ref[i].astype(jnp.float32)
    grad_x_ref[...] = total[:owned].T.astype(grad_x_ref.dtype)
    step = (rows - owned) // 2
    piece = jnp.concatenate([total[owned : owned + step], total[owned + step :]], axis=1)
    for i in range(piece_ref.shape[0]):
        piece_ref[i] = piece


def call(kernel, name, outs, in_specs, scratch=()):
    return pl.pallas_call(
        kernel,
        name=name,
        out_shape=outs,
        in_specs=in_specs,
        out_specs=jax.tree.map(lambda _: VMEM_SPEC, outs),
        scratch_shapes=list(scratch),
        compiler_params=pltpu.CompilerParams(vmem_limit_bytes=VMEM_LIMIT),
    )


def shards(features, weight, tile_vals, tile_rows, tile_cols, tile_counts, cotangent):
    bf16, f32 = jnp.bfloat16, jnp.float32
    shape = jax.ShapeDtypeStruct
    tiles = tile_vals[0, 0]
    rows, cols = tile_rows[0], tile_cols[0]
    owned, width = features.shape
    hid = weight.shape[1]
    n_row, n_plane = lax.axis_size(ROW), lax.axis_size(PLANE)
    extra = 2 * width // n_plane
    swap = [(0, 1), (1, 0)]
    slot_specs = [SMEM_SPEC, SMEM_SPEC, SMEM_SPEC, VMEM_SPEC]

    spread = jnp.broadcast_to(features[None], (n_row, owned, width))
    stripe = lax.all_to_all(spread, ROW, 0, 0)
    block = shape((n_plane, owned, width), bf16)
    keep, send = call(
        forward_kernel, "forward_tiles", (block, block), slot_specs + [VMEM_SPEC],
        [pltpu.VMEM((2 * n_plane + 1, owned, width), f32)],
    )(tile_counts, rows, cols, tiles, stripe)
    terms = (keep.astype(f32) + lax.ppermute(send, CORE, swap).astype(f32)).astype(bf16)
    terms = lax.all_to_all(terms, PLANE, 0, 0)
    hidden, payload = call(
        dense_kernel, "dense", (shape((owned, hid), bf16), shape((n_plane, owned + extra, width), bf16)),
        [VMEM_SPEC] * 3,
    )(terms, weight, cotangent)
    own = lax.all_to_all(payload, PLANE, 0, 0)
    other = lax.ppermute(own, CORE, swap)
    back = call(
        backward_kernel, "backward_tiles", shape((n_row, width + extra, owned), bf16),
        slot_specs + [VMEM_SPEC] * 2,
        [pltpu.VMEM((n_row + 1, width, owned), f32), pltpu.VMEM((2 * n_plane, width, owned), bf16)],
    )(tile_counts, rows, cols, tiles, own, other)
    back = lax.all_to_all(back, ROW, 0, 0)
    grad_x, piece = call(
        final_kernel, "final", (shape((owned, width), bf16), shape((n_plane, width // n_plane, hid), f32)),
        [VMEM_SPEC],
    )(back)
    grad_w = lax.all_to_all(piece, PLANE, 0, 0).reshape(width, hid)
    return hidden, grad_x, grad_w


def solution(mesh):
    fine = Mesh(mesh.devices.reshape(8, 4, 2, 8, 2), ROW + COL)
    placed = (
        P(ROW + COL, None),
        P(),
        P(ROW, COL, None, None, None),
        P(ROW, COL, None),
        P(ROW, COL, None),
        P(ROW, COL),
        P(ROW + COL, None),
    )
    return jax.shard_map(
        shards,
        mesh=fine,
        in_specs=placed,
        out_specs=(P(ROW + COL, None), P(ROW + COL, None), P()),
        check_vma=False,
    )
```

time: 846 us -> 182 us (0.22)
  the two profiles are of different devices: /device:TPU:4 before, /device:TPU:16 now
where the time goes in v1:
time: 182 us
  blocking collectives  109 us (60%)
  waiting for transfers between devices  37.9 us (21%)
  starting transfers between devices  26 us (14%)
  Pallas kernels  4.44 us (2%)
  local copies, waits for them, and re-layouts  2.64 us (1%)
    all_to_all x1, blocking collectives, shards(): back = lax.all_to_all(back, ROW, 0, 0)  43.7 us
    all_to_all x1, waiting for transfers between devices, shards(): stripe = lax.all_to_all(spread, ROW, 0, 0)  34 us
    all_to_all x1, blocking collectives, shards(): terms = lax.all_to_all(terms, PLANE, 0, 0)  23.3 us
    all_to_all x1, blocking collectives, shards(): own = lax.all_to_all(payload, PLANE, 0, 0)  22.2 us
    all_to_all x1, starting transfers between devices, shards(): stripe = lax.all_to_all(spread, ROW, 0, 0)  22.1 us
    all_to_all x1, blocking collectives, shards(): grad_w = lax.all_to_all(piece, PLANE, 0, 0).reshape(width, hid)  20 us
  transfers between devices with their start and end apart: 3, of which 3 were waited for; matrix products, arithmetic and copies ran while one was open for 0% of the time, Pallas kernels for 0%

profile of v1, /device:TPU:16, one launch (start us, length us, event | category | flops | bytes accessed | tf_op | source)
XLA Modules:
  0.0 181.6 jit_solution(9522172675292897992)
XLA Ops:
  0.6 2.0 %broadcast_in_dim.2 = bf16[32,128,128]{2,1,0:T(8,128)(2,1)} broadcast(bf16[128,128]{1,0:T(8,128)(2,1)} %param.7), dimensions={1,2} | broadcast | bytes 1081344 | tf_op jit(solution)/shard_map/broadcast_in_dim | solution.py:138
  2.6 0.0 copy-start
  2.6 0.0 copy-start.3
  2.6 0.0 copy-start.4
  2.6 22.1 %all-to-all-start = ((bf16[32,128,128]{2,1,0:T(8,128)(2,1)}), bf16[32,128,128]{2,1,0:T(8,128)(2,1)S(1)}, u32[]{:S(2)}, u32[]{:S(2)}) async-start(bf16[32,128,128]{2,1,0:T(8,128)(2,1)} %broadcast_in_dim.2), calls=%async_computation | async-start | bytes 2097152 | tf_op jit(solution)/shard_map/all_to_all | solution.py:139
  25.4 34.0 %all-to-all-done.stripe_ref = bf16[32,128,128]{2,1,0:T(8,128)(2,1)S(1)} async-done(((bf16[32,128,128]{2,1,0:T(8,128)(2,1)}), bf16[32,128,128]{2,1,0:T(8,128)(2,1)S(1)}, u32[]{:S(2)}, u32[]{:S(2)}) %all-to-all-start) | async-done | bytes 1048608 | tf_op jit(solution)/shard_map/all_to_all | solution.py:139
  59.4 0.0 copy-done
  59.4 0.0 copy-done.3
  59.4 0.0 copy-done.4
  59.4 1.3 forward_tiles.1
  60.8 1.9 %collective-permute-start = (bf16[16,128,128]{2,1,0:T(8,128)(2,1)S(1)}, bf16[16,128,128]{2,1,0:T(8,128)(2,1)S(1)}, u32[]{:S(2)}, u32[]{:S(2)}) collective-permute-start(bf16[16,128,128]{2,1,0:T(8,128)(2,1)S(1)} %get-tuple-element.10), channel_id=1, source_target_pairs={{0,1},{1,0},{2,3},{3,2},{4,5},{5,4},{6,7},{7,6},{8,9},{9,8},{10,11... | collective-permute-start | bytes 1572872 | tf_op jit(solution)/shard_map/ppermute | solution.py:145
  62.7 1.9 %collective-permute-done = bf16[16,128,128]{2,1,0:T(8,128)(2,1)S(1)} collective-permute-done((bf16[16,128,128]{2,1,0:T(8,128)(2,1)S(1)}, bf16[16,128,128]{2,1,0:T(8,128)(2,1)S(1)}, u32[]{:S(2)}, u32[]{:S(2)}) %collective-permute-start) | collective-permute-done | bytes 524320 | tf_op jit(solution)/shard_map/ppermute | solution.py:145
  64.6 0.0 copy-start.1
  64.6 0.0 copy-start.2
  64.6 0.1 add_convert_fusion
  64.7 23.3 %all_to_all.25.terms_ref = bf16[16,128,128]{2,1,0:T(8,128)(2,1)S(1)} all-to-all(bf16[16,128,128]{2,1,0:T(8,128)(2,1)S(1)} %add_convert_fusion), channel_id=1, replica_groups=mesh['z'=8,'x_hi'=4,'x_lo'=2,'y'=8,'core'=2] {'x_lo','y'}, dimensions={0} | all-to-all | bytes 1048576 | tf_op jit(solution)/shard_map/all_to_all | solution.py:146
  88.0 0.0 copy-done.1
  88.0 0.0 copy-done.2
  88.0 0.8 dense.1
  88.8 22.2 %all_to_all.26.own_ref = bf16[16,144,128]{2,1,0:T(8,128)(2,1)S(1)} all-to-all(bf16[16,144,128]{2,1,0:T(8,128)(2,1)S(1)} %get-tuple-element.12), channel_id=1, replica_groups=mesh['z'=8,'x_hi'=4,'x_lo'=2,'y'=8,'core'=2] {'x_lo','y'}, dimensions={0} | all-to-all | bytes 1179648 | tf_op jit(solution)/shard_map/all_to_all | solution.py:151
  111.1 1.9 %collective-permute-start.1 = (bf16[16,144,128]{2,1,0:T(8,128)(2,1)S(1)}, bf16[16,144,128]{2,1,0:T(8,128)(2,1)S(1)}, u32[]{:S(2)}, u32[]{:S(2)}) collective-permute-start(bf16[16,144,128]{2,1,0:T(8,128)(2,1)S(1)} %all_to_all.26.own_ref), channel_id=1, source_target_pairs={{0,1},{1,0},{2,3},{3,2},{4,5},{5,4},{6,7},{7,6},{8,9},{9,8},{10,11... | collective-permute-start | bytes 1769480 | tf_op jit(solution)/shard_map/ppermute | solution.py:152
  113.0 2.0 %collective-permute-done.1.other_ref = bf16[16,144,128]{2,1,0:T(8,128)(2,1)S(1)} collective-permute-done((bf16[16,144,128]{2,1,0:T(8,128)(2,1)S(1)}, bf16[16,144,128]{2,1,0:T(8,128)(2,1)S(1)}, u32[]{:S(2)}, u32[]{:S(2)}) %collective-permute-start.1) | collective-permute-done | bytes 589856 | tf_op jit(solution)/shard_map/ppermute | solution.py:152
  115.0 1.4 backward_tiles.1
  116.4 43.7 %all_to_all.27.terms_ref = bf16[32,144,128]{2,1,0:T(8,128)(2,1)S(1)} all-to-all(bf16[32,144,128]{2,1,0:T(8,128)(2,1)S(1)} %backward_tiles.1), channel_id=1, replica_groups=mesh['z'=8,'x_hi'=4,'x_lo'=2,'y'=8,'core'=2] {'z','x_hi'}, dimensions={0} | all-to-all | bytes 2359296 | tf_op jit(solution)/shard_map/all_to_all | solution.py:158
  160.1 0.9 final.1
  160.9 20.0 %all_to_all.28 = f32[16,8,256]{2,1,0:T(8,128)S(1)} all-to-all(f32[16,8,256]{2,1,0:T(8,128)S(1)} %get-tuple-element.14), channel_id=1, replica_groups=mesh['z'=8,'x_hi'=4,'x_lo'=2,'y'=8,'core'=2] {'x_lo','y'}, dimensions={0} | all-to-all | bytes 262144 | tf_op jit(solution)/shard_map/all_to_all | solution.py:163
  181.0 0.7 copy.12
Async XLA Ops:
  2.6 56.8 %copy-start = (bf16[1,1,48,128,128]{4,3,2,1,0:T(8,128)(2,1)S(1)}, bf16[1,1,48,128,128]{4,3,2,1,0:T(8,128)(2,1)}, u32[]{:S(2)}) copy-start(bf16[1,1,48,128,128]{4,3,2,1,0:T(8,128)(2,1)} %param.9) | copy-start | bytes 4718596
  2.6 56.8 %copy-start.3 = (s32[1,1,48]{2,1,0:T(1,128)S(1)}, s32[1,1,48]{2,1,0:T(1,128)}, u32[]{:S(2)}) copy-start(s32[1,1,48]{2,1,0:T(1,128)} %param.10) | copy-start | bytes 580
  2.6 56.8 %copy-start.4 = (s32[1,1,48]{2,1,0:T(1,128)S(1)}, s32[1,1,48]{2,1,0:T(1,128)}, u32[]{:S(2)}) copy-start(s32[1,1,48]{2,1,0:T(1,128)} %param.11) | copy-start | bytes 580
  2.6 56.8 %all-to-all-start = ((bf16[32,128,128]{2,1,0:T(8,128)(2,1)}), bf16[32,128,128]{2,1,0:T(8,128)(2,1)S(1)}, u32[]{:S(2)}, u32[]{:S(2)}) async-start(bf16[32,128,128]{2,1,0:T(8,128)(2,1)} %broadcast_in_dim.2), calls=%async_computation | async-start | bytes 2097152 | tf_op jit(solution)/shard_map/all_to_all | solution.py:139
  60.8 3.8 %collective-permute-start = (bf16[16,128,128]{2,1,0:T(8,128)(2,1)S(1)}, bf16[16,128,128]{2,1,0:T(8,128)(2,1)S(1)}, u32[]{:S(2)}, u32[]{:S(2)}) collective-permute-start(bf16[16,128,128]{2,1,0:T(8,128)(2,1)S(1)} %get-tuple-element.10), channel_id=1, source_target_pairs={{0,1},{1,0},{2,3},{3,2},{4,5},{5,4},{6,7},{7,6},{8,9},{9,8},{10,11... | collective-permute-start | bytes 1572872 | tf_op jit(solution)/shard_map/ppermute | solution.py:145
  64.6 23.4 %copy-start.1 = (bf16[128,256]{1,0:T(8,128)(2,1)S(1)}, bf16[128,256]{1,0:T(8,128)(2,1)}, u32[]{:S(2)}) copy-start(bf16[128,256]{1,0:T(8,128)(2,1)} %weight_ref.1) | copy-start | bytes 196612
  64.6 23.4 %copy-start.2 = (bf16[128,256]{1,0:T(8,128)(2,1)S(1)}, bf16[128,256]{1,0:T(8,128)(2,1)}, u32[]{:S(2)}) copy-start(bf16[128,256]{1,0:T(8,128)(2,1)} %cot_ref.1) | copy-start | bytes 196612
  111.1 3.9 %collective-permute-start.1 = (bf16[16,144,128]{2,1,0:T(8,128)(2,1)S(1)}, bf16[16,144,128]{2,1,0:T(8,128)(2,1)S(1)}, u32[]{:S(2)}, u32[]{:S(2)}) collective-permute-start(bf16[16,144,128]{2,1,0:T(8,128)(2,1)S(1)} %all_to_all.26.own_ref), channel_id=1, source_target_pairs={{0,1},{1,0},{2,3},{3,2},{4,5},{5,4},{6,7},{7,6},{8,9},{9,8},{10,11... | collective-permute-start | bytes 1769480 | tf_op jit(solution)/shard_map/ppermute | solution.py:152

commit v2 on v1

--- a/solution.py
+++ b/solution.py
@@ -7,7 +7,9 @@
 from jax.experimental.pallas import tpu as pltpu
 from jax.sharding import Mesh, PartitionSpec as P
 
-ROW = ("z", "x_hi")
+ROW = ("zb", "za", "xb", "xa")
+Z = ("zb", "za")
+GROUP = ("zb", "xb", "xa")
 PLANE = ("x_lo", "y")
 CORE = "core"
 COL = PLANE + (CORE,)
@@ -18,11 +20,15 @@
 VMEM_SPEC = pl.BlockSpec(memory_space=pltpu.VMEM)
 
 
-def place(block, core):
+def row_place(block, core):
     return ((block & 1) ^ core) * 16 + (block >> 1)
 
 
-def add_tiles(count, slots, out_place, product, acc):
+def col_place(block, za):
+    return (((block >> 2) & 1) ^ za) * 16 + ((block >> 3) * 4 + (block & 3))
+
+
+def add_tiles(count, out_place, product, acc):
     spare = acc.shape[0] - 1
 
     def group(index, carry):
@@ -37,16 +43,21 @@
     lax.fori_loop(0, (count + UNROLL - 1) // UNROLL, group, 0)
 
 
-def forward_kernel(count_ref, rows_ref, cols_ref, tiles_ref, stripe_ref, keep_ref, send_ref, acc):
-    core = lax.axis_index(CORE)
+def forward_kernel(count_ref, rows_ref, cols_ref, tiles_ref, own_ref, low_ref, high_ref, keep_ref, send_ref, acc, stripe):
+    core, za = lax.axis_index(CORE), lax.axis_index("za")
+    half, part = own_ref.shape[0], low_ref.shape[0]
+    stripe[:half] = own_ref[...]
+    stripe[half : half + part] = low_ref[...]
+    stripe[half + part :] = high_ref[...]
     acc[...] = jnp.zeros_like(acc)
 
     def product(k):
-        return jnp.dot(tiles_ref[k], stripe_ref[cols_ref[0, k]], preferred_element_type=jnp.float32)
-
-    add_tiles(count_ref[0, 0], tiles_ref.shape[0], lambda k: place(rows_ref[0, k], core), product, acc)
+        features = stripe[col_place(cols_ref[0, k], za)]
+        return jnp.dot(tiles_ref[k], features, preferred_element_type=jnp.float32)
+
+    add_tiles(count_ref[0, 0], lambda k: row_place(rows_ref[0, k], core), product, acc)
     half = keep_ref.shape[0]
-    keep_ref[...] = acc[:half].astype(keep_ref.dtype)
+    keep_ref[...] = acc[:half]
     send_ref[...] = acc[half : 2 * half].astype(send_ref.dtype)
 
 
@@ -78,8 +89,10 @@
         payload_ref[i, owned:] = packed.astype(jnp.bfloat16)
 
 
-def backward_kernel(count_ref, rows_ref, cols_ref, tiles_ref, own_ref, other_ref, out_ref, acc, stripe):
-    core = lax.axis_index(CORE)
+def backward_kernel(
+    count_ref, rows_ref, cols_ref, tiles_ref, own_ref, other_ref, keep_ref, grad_ref, up_ref, down_ref, acc, stripe
+):
+    core, za = lax.axis_index(CORE), lax.axis_index("za")
     half = own_ref.shape[0]
     owned = stripe.shape[1]
     stripe[:half] = own_ref[:, :owned]
@@ -87,15 +100,29 @@
     acc[...] = jnp.zeros_like(acc)
 
     def product(k):
-        return jnp.dot(stripe[place(rows_ref[0, k], core)], tiles_ref[k], preferred_element_type=jnp.float32)
-
-    add_tiles(count_ref[0, 0], tiles_ref.shape[0], lambda k: cols_ref[0, k], product, acc)
+        upstream = stripe[row_place(rows_ref[0, k], core)]
+        return jnp.dot(upstream, tiles_ref[k], preferred_element_type=jnp.float32)
+
+    add_tiles(count_ref[0, 0], lambda k: col_place(cols_ref[0, k], za), product, acc)
     grad = own_ref[0, owned:].astype(jnp.float32) + other_ref[0, owned:].astype(jnp.float32)
     for i in range(1, half):
         grad += own_ref[i, owned:].astype(jnp.float32) + other_ref[i, owned:].astype(jnp.float32)
-    grad = grad.astype(out_ref.dtype)
-    for i in range(out_ref.shape[0]):
-        out_ref[i, :owned] = acc[i].astype(out_ref.dtype)
+    grad_ref[...] = grad
+    half = keep_ref.shape[0]
+    keep_ref[...] = acc[:half]
+    for i in range(half // 2):
+        up_ref[i * owned : (i + 1) * owned] = acc[half + i].astype(up_ref.dtype)
+        down_ref[i * owned : (i + 1) * owned] = acc[half + half // 2 + i].astype(down_ref.dtype)
+    up_ref[half // 2 * owned :] = grad.astype(up_ref.dtype)
+
+
+def middle_kernel(keep_ref, grad_ref, low_ref, high_ref, out_ref):
+    half, owned, _ = keep_ref.shape
+    part = half // 2
+    grad = (grad_ref[...] + low_ref[part * owned :].astype(jnp.float32)).astype(out_ref.dtype)
+    for i in range(half):
+        came = (low_ref if i < part else high_ref)[i % part * owned : (i % part + 1) * owned]
+        out_ref[i, :owned] = (keep_ref[i] + came.astype(jnp.float32)).astype(out_ref.dtype)
         out_ref[i, owned:] = grad
 
 
@@ -131,33 +158,57 @@
     owned, width = features.shape
     hid = weight.shape[1]
     n_row, n_plane = lax.axis_size(ROW), lax.axis_size(PLANE)
+    half, part = n_row // 2, n_row // 4
     extra = 2 * width // n_plane
     swap = [(0, 1), (1, 0)]
-    slot_specs = [SMEM_SPEC, SMEM_SPEC, SMEM_SPEC, VMEM_SPEC]
-
-    spread = jnp.broadcast_to(features[None], (n_row, owned, width))
-    stripe = lax.all_to_all(spread, ROW, 0, 0)
-    block = shape((n_plane, owned, width), bf16)
+    n_z = lax.axis_size(Z)
+    up = [(i, (i + 1) % n_z) for i in range(n_z)]
+    down = [(i, (i - 1) % n_z) for i in range(n_z)]
+    tile_specs = [SMEM_SPEC] * 3 + [VMEM_SPEC] * 3
+
+    spread = jnp.broadcast_to(features[None], (half, owned, width))
+    own = lax.all_to_all(spread, GROUP, 0, 0)
+    low = lax.ppermute(own[:part], Z, up)
+    high = lax.ppermute(own[part:], Z, down)
     keep, send = call(
-        forward_kernel, "forward_tiles", (block, block), slot_specs + [VMEM_SPEC],
-        [pltpu.VMEM((2 * n_plane + 1, owned, width), f32)],
-    )(tile_counts, rows, cols, tiles, stripe)
-    terms = (keep.astype(f32) + lax.ppermute(send, CORE, swap).astype(f32)).astype(bf16)
+        forward_kernel,
+        "forward_tiles",
+        (shape((n_plane, owned, width), f32), shape((n_plane, owned, width), bf16)),
+        tile_specs + [VMEM_SPEC],
+        [pltpu.VMEM((2 * n_plane + 1, owned, width), f32), pltpu.VMEM((n_row, owned, width), bf16)],
+    )(tile_counts, rows, cols, tiles, own, low, high)
+    terms = (keep + lax.ppermute(send, CORE, swap).astype(f32)).astype(bf16)
     terms = lax.all_to_all(terms, PLANE, 0, 0)
     hidden, payload = call(
-        dense_kernel, "dense", (shape((owned, hid), bf16), shape((n_plane, owned + extra, width), bf16)),
+        dense_kernel,
+        "dense",
+        (shape((owned, hid), bf16), shape((n_plane, owned + extra, width), bf16)),
         [VMEM_SPEC] * 3,
     )(terms, weight, cotangent)
     own = lax.all_to_all(payload, PLANE, 0, 0)
     other = lax.ppermute(own, CORE, swap)
-    back = call(
-        backward_kernel, "backward_tiles", shape((n_row, width + extra, owned), bf16),
-        slot_specs + [VMEM_SPEC] * 2,
+    keep, grad, to_up, to_down = call(
+        backward_kernel,
+        "backward_tiles",
+        (
+            shape((half, width, owned), f32),
+            shape((extra, width), f32),
+            shape((part * width + extra, owned), bf16),
+            shape((part * width, owned), bf16),
+        ),
+        tile_specs,
         [pltpu.VMEM((n_row + 1, width, owned), f32), pltpu.VMEM((2 * n_plane, width, owned), bf16)],
     )(tile_counts, rows, cols, tiles, own, other)
-    back = lax.all_to_all(back, ROW, 0, 0)
+    low = lax.ppermute(to_up, Z, up)
+    high = lax.ppermute(to_down, Z, down)
+    back = call(middle_kernel, "middle", shape((half, width + extra, owned), bf16), [VMEM_SPEC] * 4)(
+        keep, grad, low, high
+    )
+    back = lax.all_to_all(back, GROUP, 0, 0)
     grad_x, piece = call(
-        final_kernel, "final", (shape((owned, width), bf16), shape((n_plane, width // n_plane, hid), f32)),
+        final_kernel,
+        "final",
+        (shape((owned, width), bf16), shape((n_plane, width // n_plane, hid), f32)),
         [VMEM_SPEC],
     )(back)
     grad_w = lax.all_to_all(piece, PLANE, 0, 0).reshape(width, hid)
@@ -165,7 +216,7 @@
 
 
 def solution(mesh):
-    fine = Mesh(mesh.devices.reshape(8, 4, 2, 8, 2), ROW + COL)
+    fine = Mesh(mesh.devices.reshape(4, 2, 2, 2, 2, 8, 2), ROW + COL)
     placed = (
         P(ROW + COL, None),
         P(),

time: 182 us -> 172 us (0.945)
  waiting for transfers between devices: 37.9 us -> 16.3 us
  blocking collectives: 109 us -> 130 us
  starting transfers between devices: 26 us -> 17.8 us
    all_to_all x1 -> x0, waiting for transfers between devices: 34 us -> none  [shards(): stripe = lax.all_to_all(spread, ROW, 0, 0)]
    all_to_all x1 -> x2, blocking collectives: 43.7 us -> 71.2 us  [the longest x1 40.3 us: shards(): own = lax.all_to_all(spread, GROUP, 0, 0)]
    all_to_all x1 -> x0, starting transfers between devices: 22.1 us -> none  [shards(): stripe = lax.all_to_all(spread, ROW, 0, 0)]
    ppermute x1 -> x5, starting transfers between devices: 1.92 us -> 15.9 us  [the longest x1 5.13 us: shards(): high = lax.ppermute(to_down, Z, down)]
    ppermute x1 -> x5, waiting for transfers between devices: 1.88 us -> 14.3 us  [the longest x1 5.56 us: shards(): high = lax.ppermute(to_down, Z, down)]
    all_to_all x1, blocking collectives: 20 us -> 12.1 us  [shards(): grad_w = lax.all_to_all(piece, PLANE, 0, 0).reshape(width, hid)]
  transfers between devices with their start and end apart: 3 -> 6, of which waited for: 3 -> 5; matrix products, arithmetic and copies ran while one was open for 0% -> 0% of each run, Pallas kernels for 0% -> 0%
where the time goes in v2:
time: 172 us; the launch traced here: 171 us
  blocking collectives  130 us (76%)
  starting transfers between devices  17.8 us (10%)
  waiting for transfers between devices  16.3 us (9%)
  Pallas kernels  4.18 us (2%)
    all_to_all x1, blocking collectives, shards(): own = lax.all_to_all(spread, GROUP, 0, 0)  40.3 us
    all_to_all x1, blocking collectives, shards(): back = lax.all_to_all(back, GROUP, 0, 0)  30.9 us
    all_to_all x1, blocking collectives, shards(): terms = lax.all_to_all(terms, PLANE, 0, 0)  24 us
    all_to_all x1, blocking collectives, shards(): own = lax.all_to_all(payload, PLANE, 0, 0)  22.2 us
    all_to_all x1, blocking collectives, shards(): grad_w = lax.all_to_all(piece, PLANE, 0, 0).reshape(width, hid)  12.1 us
    ppermute x1, waiting for transfers between devices, shards(): high = lax.ppermute(to_down, Z, down)  5.56 us
    ppermute x1, waiting for transfers between devices, shards(): low = lax.ppermute(own[:part], Z, up)  5.2 us
    ppermute x1, starting transfers between devices, shards(): high = lax.ppermute(to_down, Z, down)  5.13 us
  transfers between devices with their start and end apart: 6, of which 5 were waited for; matrix products, arithmetic and copies ran while one was open for 0% of the time, Pallas kernels for 0%

profile of v2, /device:TPU:16, one launch (start us, length us, event | category | flops | bytes accessed | tf_op | source)
XLA Modules:
  0.0 171.1 jit_solution(15908912818877716773)
XLA Ops:
  0.6 0.0 copy-start.4
  0.6 0.0 copy-start.3
  0.7 0.0 copy-start
  0.7 1.0 broadcast_in_dim.2
  1.6 40.3 %all_to_all.25.own_ref = bf16[16,128,128]{2,1,0:T(8,128)(2,1)S(1)} all-to-all(bf16[16,128,128]{2,1,0:T(8,128)(2,1)S(1)} %broadcast_in_dim.2), channel_id=1, replica_groups=mesh['zb'=4,'za'=2,'xb'=2,'xa'=2,'x_lo'=2,'y'=8,'core'=2] {'zb','xb','xa'}, dimensions={0} | all-to-all | bytes 1048576 | tf_op jit(solution)/shard_map/all_to_all | solution.py:170
  42.0 5.0 %collective-permute-start.1 = (bf16[8,128,128]{2,1,0:T(8,128)(2,1)S(1)}, bf16[8,128,128]{2,1,0:T(8,128)(2,1)S(1)}, u32[]{:S(2)}, u32[]{:S(2)}) collective-permute-start(bf16[8,128,128]{2,1,0:T(8,128)(2,1)S(1)} %get-tuple-element.23), channel_id=1, source_target_pairs={{0,896},{128,0},{256,128},{384,256},{512,384},{640,512},{768,640},... | collective-permute-start | bytes 786440 | tf_op jit(solution)/shard_map/ppermute | solution.py:172
  47.1 1.9 %collective-permute-start = (bf16[8,128,128]{2,1,0:T(8,128)(2,1)S(1)}, bf16[8,128,128]{2,1,0:T(8,128)(2,1)S(1)}, u32[]{:S(2)}, u32[]{:S(2)}) collective-permute-start(bf16[8,128,128]{2,1,0:T(8,128)(2,1)S(1)} %get-tuple-element.24), channel_id=1, source_target_pairs={{0,128},{128,256},{256,384},{384,512},{512,640},{640,768},{768,896... | collective-permute-start | bytes 786440 | tf_op jit(solution)/shard_map/ppermute | solution.py:171
  49.6 1.7 collective-permute-done.1.high_ref
  51.3 5.2 %collective-permute-done.low_ref = bf16[8,128,128]{2,1,0:T(8,128)(2,1)S(1)} collective-permute-done((bf16[8,128,128]{2,1,0:T(8,128)(2,1)S(1)}, bf16[8,128,128]{2,1,0:T(8,128)(2,1)S(1)}, u32[]{:S(2)}, u32[]{:S(2)}) %collective-permute-start) | collective-permute-done | bytes 262176 | tf_op jit(solution)/shard_map/ppermute | solution.py:171
  56.5 0.0 copy-done.4
  56.5 0.0 copy-done.3
  56.5 0.0 copy-done
  56.5 1.2 forward_tiles.1
  57.8 1.9 %collective-permute-start.2 = (bf16[16,128,128]{2,1,0:T(8,128)(2,1)S(1)}, bf16[16,128,128]{2,1,0:T(8,128)(2,1)S(1)}, u32[]{:S(2)}, u32[]{:S(2)}) collective-permute-start(bf16[16,128,128]{2,1,0:T(8,128)(2,1)S(1)} %get-tuple-element.14), channel_id=1, source_target_pairs={{0,1},{1,0},{2,3},{3,2},{4,5},{5,4},{6,7},{7,6},{8,9},{9,8},{10,11... | collective-permute-start | bytes 1572872 | tf_op jit(solution)/shard_map/ppermute | solution.py:180
  59.7 1.9 %collective-permute-done.2 = bf16[16,128,128]{2,1,0:T(8,128)(2,1)S(1)} collective-permute-done((bf16[16,128,128]{2,1,0:T(8,128)(2,1)S(1)}, bf16[16,128,128]{2,1,0:T(8,128)(2,1)S(1)}, u32[]{:S(2)}, u32[]{:S(2)}) %collective-permute-start.2) | collective-permute-done | bytes 524320 | tf_op jit(solution)/shard_map/ppermute | solution.py:180
  61.6 0.0 copy-start.1
  61.6 0.0 copy-start.2
  61.6 0.1 add_convert_fusion
  61.7 24.0 %all_to_all.26.terms_ref = bf16[16,128,128]{2,1,0:T(8,128)(2,1)S(1)} all-to-all(bf16[16,128,128]{2,1,0:T(8,128)(2,1)S(1)} %add_convert_fusion), channel_id=1, replica_groups=mesh['zb'=4,'za'=2,'xb'=2,'xa'=2,'x_lo'=2,'y'=8,'core'=2] {'x_lo','y'}, dimensions={0} | all-to-all | bytes 1048576 | tf_op jit(solution)/shard_map/all_to_all | solution.py:181
  85.8 0.0 copy-done.1
  85.8 0.0 copy-done.2
  85.8 0.8 dense.1
  86.6 22.2 %all_to_all.27.own_ref = bf16[16,144,128]{2,1,0:T(8,128)(2,1)S(1)} all-to-all(bf16[16,144,128]{2,1,0:T(8,128)(2,1)S(1)} %get-tuple-element.16), channel_id=1, replica_groups=mesh['zb'=4,'za'=2,'xb'=2,'xa'=2,'x_lo'=2,'y'=8,'core'=2] {'x_lo','y'}, dimensions={0} | all-to-all | bytes 1179648 | tf_op jit(solution)/shard_map/all_to_all | solution.py:188
  108.8 1.9 %collective-permute-start.3 = (bf16[16,144,128]{2,1,0:T(8,128)(2,1)S(1)}, bf16[16,144,128]{2,1,0:T(8,128)(2,1)S(1)}, u32[]{:S(2)}, u32[]{:S(2)}) collective-permute-start(bf16[16,144,128]{2,1,0:T(8,128)(2,1)S(1)} %all_to_all.27.own_ref), channel_id=1, source_target_pairs={{0,1},{1,0},{2,3},{3,2},{4,5},{5,4},{6,7},{7,6},{8,9},{9,8},{10,11... | collective-permute-start | bytes 1769480 | tf_op jit(solution)/shard_map/ppermute | solution.py:189
  110.8 2.0 %collective-permute-done.3.other_ref = bf16[16,144,128]{2,1,0:T(8,128)(2,1)S(1)} collective-permute-done((bf16[16,144,128]{2,1,0:T(8,128)(2,1)S(1)}, bf16[16,144,128]{2,1,0:T(8,128)(2,1)S(1)}, u32[]{:S(2)}, u32[]{:S(2)}) %collective-permute-start.3) | collective-permute-done | bytes 589856 | tf_op jit(solution)/shard_map/ppermute | solution.py:189
  112.7 1.2 backward_tiles.1
  114.0 1.9 %collective-permute-start.4 = (bf16[1040,128]{1,0:T(8,128)(2,1)S(1)}, bf16[1040,128]{1,0:T(8,128)(2,1)S(1)}, u32[]{:S(2)}, u32[]{:S(2)}) collective-permute-start(bf16[1040,128]{1,0:T(8,128)(2,1)S(1)} %get-tuple-element.19), channel_id=1, source_target_pairs={{0,128},{128,256},{256,384},{384,512},{512,640},{640,768},{768,896... | collective-permute-start | bytes 798728 | tf_op jit(solution)/shard_map/ppermute | solution.py:202
  115.9 5.1 %collective-permute-start.5 = (bf16[1024,128]{1,0:T(8,128)(2,1)S(1)}, bf16[1024,128]{1,0:T(8,128)(2,1)S(1)}, u32[]{:S(2)}, u32[]{:S(2)}) collective-permute-start(bf16[1024,128]{1,0:T(8,128)(2,1)S(1)} %get-tuple-element.20), channel_id=1, source_target_pairs={{0,896},{128,0},{256,128},{384,256},{512,384},{640,512},{768,640},... | collective-permute-start | bytes 786440 | tf_op jit(solution)/shard_map/ppermute | solution.py:203
  121.0 5.6 %collective-permute-done.5.high_ref = bf16[1024,128]{1,0:T(8,128)(2,1)S(1)} collective-permute-done((bf16[1024,128]{1,0:T(8,128)(2,1)S(1)}, bf16[1024,128]{1,0:T(8,128)(2,1)S(1)}, u32[]{:S(2)}, u32[]{:S(2)}) %collective-permute-start.5) | collective-permute-done | bytes 262176 | tf_op jit(solution)/shard_map/ppermute | solution.py:203
  126.6 0.0 collective-permute-done.4.low_ref
  126.6 0.1 middle.1
  126.7 30.9 %all_to_all.28.terms_ref = bf16[16,144,128]{2,1,0:T(8,128)(2,1)S(1)} all-to-all(bf16[16,144,128]{2,1,0:T(8,128)(2,1)S(1)} %middle.1), channel_id=1, replica_groups=mesh['zb'=4,'za'=2,'xb'=2,'xa'=2,'x_lo'=2,'y'=8,'core'=2] {'zb','xb','xa'}, dimensions={0} | all-to-all | bytes 1179648 | tf_op jit(solution)/shard_map/all_to_all | solution.py:207
  157.6 0.8 final.1
  158.3 12.1 %all_to_all.29 = f32[16,8,256]{2,1,0:T(8,128)S(1)} all-to-all(f32[16,8,256]{2,1,0:T(8,128)S(1)} %get-tuple-element.22), channel_id=1, replica_groups=mesh['zb'=4,'za'=2,'xb'=2,'xa'=2,'x_lo'=2,'y'=8,'core'=2] {'x_lo','y'}, dimensions={0} | all-to-all | bytes 262144 | tf_op jit(solution)/shard_map/all_to_all | solution.py:214
  170.5 0.7 copy.12
  (1 shorter events, 0.0 us)
Async XLA Ops:
  0.6 55.9 %copy-start.4 = (s32[1,1,48]{2,1,0:T(1,128)S(1)}, s32[1,1,48]{2,1,0:T(1,128)}, u32[]{:S(2)}) copy-start(s32[1,1,48]{2,1,0:T(1,128)} %param.11) | copy-start | bytes 580
  0.6 55.9 %copy-start.3 = (s32[1,1,48]{2,1,0:T(1,128)S(1)}, s32[1,1,48]{2,1,0:T(1,128)}, u32[]{:S(2)}) copy-start(s32[1,1,48]{2,1,0:T(1,128)} %param.10) | copy-start | bytes 580
  0.7 55.9 %copy-start = (bf16[1,1,48,128,128]{4,3,2,1,0:T(8,128)(2,1)S(1)}, bf16[1,1,48,128,128]{4,3,2,1,0:T(8,128)(2,1)}, u32[]{:S(2)}) copy-start(bf16[1,1,48,128,128]{4,3,2,1,0:T(8,128)(2,1)} %param.9) | copy-start | bytes 4718596
  42.0 9.3 %collective-permute-start.1 = (bf16[8,128,128]{2,1,0:T(8,128)(2,1)S(1)}, bf16[8,128,128]{2,1,0:T(8,128)(2,1)S(1)}, u32[]{:S(2)}, u32[]{:S(2)}) collective-permute-start(bf16[8,128,128]{2,1,0:T(8,128)(2,1)S(1)} %get-tuple-element.23), channel_id=1, source_target_pairs={{0,896},{128,0},{256,128},{384,256},{512,384},{640,512},{768,640},... | collective-permute-start | bytes 786440 | tf_op jit(solution)/shard_map/ppermute | solution.py:172
  47.1 9.5 %collective-permute-start = (bf16[8,128,128]{2,1,0:T(8,128)(2,1)S(1)}, bf16[8,128,128]{2,1,0:T(8,128)(2,1)S(1)}, u32[]{:S(2)}, u32[]{:S(2)}) collective-permute-start(bf16[8,128,128]{2,1,0:T(8,128)(2,1)S(1)} %get-tuple-element.24), channel_id=1, source_target_pairs={{0,128},{128,256},{256,384},{384,512},{512,640},{640,768},{768,896... | collective-permute-start | bytes 786440 | tf_op jit(solution)/shard_map/ppermute | solution.py:171
  57.8 3.8 %collective-permute-start.2 = (bf16[16,128,128]{2,1,0:T(8,128)(2,1)S(1)}, bf16[16,128,128]{2,1,0:T(8,128)(2,1)S(1)}, u32[]{:S(2)}, u32[]{:S(2)}) collective-permute-start(bf16[16,128,128]{2,1,0:T(8,128)(2,1)S(1)} %get-tuple-element.14), channel_id=1, source_target_pairs={{0,1},{1,0},{2,3},{3,2},{4,5},{5,4},{6,7},{7,6},{8,9},{9,8},{10,11... | collective-permute-start | bytes 1572872 | tf_op jit(solution)/shard_map/ppermute | solution.py:180
  61.6 24.2 %copy-start.1 = (bf16[128,256]{1,0:T(8,128)(2,1)S(1)}, bf16[128,256]{1,0:T(8,128)(2,1)}, u32[]{:S(2)}) copy-start(bf16[128,256]{1,0:T(8,128)(2,1)} %weight_ref.1) | copy-start | bytes 196612
  61.6 24.2 %copy-start.2 = (bf16[128,256]{1,0:T(8,128)(2,1)S(1)}, bf16[128,256]{1,0:T(8,128)(2,1)}, u32[]{:S(2)}) copy-start(bf16[128,256]{1,0:T(8,128)(2,1)} %cot_ref.1) | copy-start | bytes 196612
  108.8 3.9 %collective-permute-start.3 = (bf16[16,144,128]{2,1,0:T(8,128)(2,1)S(1)}, bf16[16,144,128]{2,1,0:T(8,128)(2,1)S(1)}, u32[]{:S(2)}, u32[]{:S(2)}) collective-permute-start(bf16[16,144,128]{2,1,0:T(8,128)(2,1)S(1)} %all_to_all.27.own_ref), channel_id=1, source_target_pairs={{0,1},{1,0},{2,3},{3,2},{4,5},{5,4},{6,7},{7,6},{8,9},{9,8},{10,11... | collective-permute-start | bytes 1769480 | tf_op jit(solution)/shard_map/ppermute | solution.py:189
  114.0 12.6 %collective-permute-start.4 = (bf16[1040,128]{1,0:T(8,128)(2,1)S(1)}, bf16[1040,128]{1,0:T(8,128)(2,1)S(1)}, u32[]{:S(2)}, u32[]{:S(2)}) collective-permute-start(bf16[1040,128]{1,0:T(8,128)(2,1)S(1)} %get-tuple-element.19), channel_id=1, source_target_pairs={{0,128},{128,256},{256,384},{384,512},{512,640},{640,768},{768,896... | collective-permute-start | bytes 798728 | tf_op jit(solution)/shard_map/ppermute | solution.py:202
  115.9 10.7 %collective-permute-start.5 = (bf16[1024,128]{1,0:T(8,128)(2,1)S(1)}, bf16[1024,128]{1,0:T(8,128)(2,1)S(1)}, u32[]{:S(2)}, u32[]{:S(2)}) collective-permute-start(bf16[1024,128]{1,0:T(8,128)(2,1)S(1)} %get-tuple-element.20), channel_id=1, source_target_pairs={{0,896},{128,0},{256,128},{384,256},{512,384},{640,512},{768,640},... | collective-permute-start | bytes 786440 | tf_op jit(solution)/shard_map/ppermute | solution.py:203

commit v3 on v2

--- a/solution.py
+++ b/solution.py
@@ -9,11 +9,11 @@
 
 ROW = ("zb", "za", "xb", "xa")
 Z = ("zb", "za")
-GROUP = ("zb", "xb", "xa")
+GROUP = ("xb", "xa", "zb")
 PLANE = ("x_lo", "y")
 CORE = "core"
 COL = PLANE + (CORE,)
-UNROLL = 4
+UNROLL = 16
 VMEM_LIMIT = 32 * 1024 * 1024
 
 SMEM_SPEC = pl.BlockSpec(memory_space=pltpu.SMEM)
@@ -25,7 +25,7 @@
 
 
 def col_place(block, za):
-    return (((block >> 2) & 1) ^ za) * 16 + ((block >> 3) * 4 + (block & 3))
+    return (((block >> 2) & 1) ^ za) * 16 + ((block & 3) * 4 + (block >> 3))
 
 
 def add_tiles(count, out_place, product, acc):

time: 172 us -> 172 us (level)
    ppermute x1, starting transfers between devices: 5.03 us -> 3.3 us  [shards(): high = lax.ppermute(own[part:], Z, down)]
where the time goes in v3:
time: 172 us; the launch traced here: 171 us
  blocking collectives  130 us (76%)
  starting transfers between devices  16.9 us (10%)
  waiting for transfers between devices  16 us (9%)
  Pallas kernels  4.71 us (3%)
    all_to_all x1, blocking collectives, shards(): own = lax.all_to_all(spread, GROUP, 0, 0)  41.8 us
    all_to_all x1, blocking collectives, shards(): back = lax.all_to_all(back, GROUP, 0, 0)  30.1 us
    all_to_all x1, blocking collectives, shards(): terms = lax.all_to_all(terms, PLANE, 0, 0)  23.4 us
    all_to_all x1, blocking collectives, shards(): own = lax.all_to_all(payload, PLANE, 0, 0)  22.2 us
    all_to_all x1, blocking collectives, shards(): grad_w = lax.all_to_all(piece, PLANE, 0, 0).reshape(width, hid)  12.6 us
    ppermute x1, waiting for transfers between devices, shards(): high = lax.ppermute(to_down, Z, down)  5.56 us
    ppermute x1, starting transfers between devices, shards(): high = lax.ppermute(to_down, Z, down)  5.13 us
    ppermute x1, waiting for transfers between devices, shards(): low = lax.ppermute(own[:part], Z, up)  3.88 us
  transfers between devices with their start and end apart: 6, of which 5 were waited for; matrix products, arithmetic and copies ran while one was open for 0% of the time, Pallas kernels for 0%

profile of v3, /device:TPU:16, one launch (start us, length us, event | category | flops | bytes accessed | tf_op | source)
XLA Modules:
  0.0 171.0 jit_solution(5969791439827274154)
XLA Ops:
  0.6 0.0 copy-start.4
  0.6 0.0 copy-start.3
  0.7 0.0 copy-start
  0.7 1.0 broadcast_in_dim.2
  1.6 41.8 %all_to_all.25.own_ref = bf16[16,128,128]{2,1,0:T(8,128)(2,1)S(1)} all-to-all(bf16[16,128,128]{2,1,0:T(8,128)(2,1)S(1)} %broadcast_in_dim.2), channel_id=1, replica_groups=mesh['zb'=4,'za'=2,'xb'=2,'xa'=2,'x_lo'=2,'y'=8,'core'=2] {'xb','xa','zb'}, dimensions={0} | all-to-all | bytes 1048576 | tf_op jit(solution)/shard_map/all_to_all | solution.py:170
  43.5 3.3 %collective-permute-start.1 = (bf16[8,128,128]{2,1,0:T(8,128)(2,1)S(1)}, bf16[8,128,128]{2,1,0:T(8,128)(2,1)S(1)}, u32[]{:S(2)}, u32[]{:S(2)}) collective-permute-start(bf16[8,128,128]{2,1,0:T(8,128)(2,1)S(1)} %get-tuple-element.23), channel_id=1, source_target_pairs={{0,896},{128,0},{256,128},{384,256},{512,384},{640,512},{768,640},... | collective-permute-start | bytes 786440 | tf_op jit(solution)/shard_map/ppermute | solution.py:172
  46.8 2.7 %collective-permute-start = (bf16[8,128,128]{2,1,0:T(8,128)(2,1)S(1)}, bf16[8,128,128]{2,1,0:T(8,128)(2,1)S(1)}, u32[]{:S(2)}, u32[]{:S(2)}) collective-permute-start(bf16[8,128,128]{2,1,0:T(8,128)(2,1)S(1)} %get-tuple-element.24), channel_id=1, source_target_pairs={{0,128},{128,256},{256,384},{384,512},{512,640},{640,768},{768,896... | collective-permute-start | bytes 786440 | tf_op jit(solution)/shard_map/ppermute | solution.py:171
  50.2 2.8 %collective-permute-done.1.high_ref = bf16[8,128,128]{2,1,0:T(8,128)(2,1)S(1)} collective-permute-done((bf16[8,128,128]{2,1,0:T(8,128)(2,1)S(1)}, bf16[8,128,128]{2,1,0:T(8,128)(2,1)S(1)}, u32[]{:S(2)}, u32[]{:S(2)}) %collective-permute-start.1) | collective-permute-done | bytes 262176 | tf_op jit(solution)/shard_map/ppermute | solution.py:172
  52.9 3.9 %collective-permute-done.low_ref = bf16[8,128,128]{2,1,0:T(8,128)(2,1)S(1)} collective-permute-done((bf16[8,128,128]{2,1,0:T(8,128)(2,1)S(1)}, bf16[8,128,128]{2,1,0:T(8,128)(2,1)S(1)}, u32[]{:S(2)}, u32[]{:S(2)}) %collective-permute-start) | collective-permute-done | bytes 262176 | tf_op jit(solution)/shard_map/ppermute | solution.py:171
  56.8 0.0 copy-done.4
  56.8 0.0 copy-done.3
  56.8 0.0 copy-done
  56.8 1.5 forward_tiles.1
  58.3 1.9 %collective-permute-start.2 = (bf16[16,128,128]{2,1,0:T(8,128)(2,1)S(1)}, bf16[16,128,128]{2,1,0:T(8,128)(2,1)S(1)}, u32[]{:S(2)}, u32[]{:S(2)}) collective-permute-start(bf16[16,128,128]{2,1,0:T(8,128)(2,1)S(1)} %get-tuple-element.14), channel_id=1, source_target_pairs={{0,1},{1,0},{2,3},{3,2},{4,5},{5,4},{6,7},{7,6},{8,9},{9,8},{10,11... | collective-permute-start | bytes 1572872 | tf_op jit(solution)/shard_map/ppermute | solution.py:180
  60.3 1.9 %collective-permute-done.2 = bf16[16,128,128]{2,1,0:T(8,128)(2,1)S(1)} collective-permute-done((bf16[16,128,128]{2,1,0:T(8,128)(2,1)S(1)}, bf16[16,128,128]{2,1,0:T(8,128)(2,1)S(1)}, u32[]{:S(2)}, u32[]{:S(2)}) %collective-permute-start.2) | collective-permute-done | bytes 524320 | tf_op jit(solution)/shard_map/ppermute | solution.py:180
  62.1 0.0 copy-start.1
  62.1 0.0 copy-start.2
  62.1 0.1 add_convert_fusion
  62.3 23.4 %all_to_all.26.terms_ref = bf16[16,128,128]{2,1,0:T(8,128)(2,1)S(1)} all-to-all(bf16[16,128,128]{2,1,0:T(8,128)(2,1)S(1)} %add_convert_fusion), channel_id=1, replica_groups=mesh['zb'=4,'za'=2,'xb'=2,'xa'=2,'x_lo'=2,'y'=8,'core'=2] {'x_lo','y'}, dimensions={0} | all-to-all | bytes 1048576 | tf_op jit(solution)/shard_map/all_to_all | solution.py:181
  85.7 0.0 copy-done.1
  85.7 0.0 copy-done.2
  85.7 0.8 dense.1
  86.6 22.2 %all_to_all.27.own_ref = bf16[16,144,128]{2,1,0:T(8,128)(2,1)S(1)} all-to-all(bf16[16,144,128]{2,1,0:T(8,128)(2,1)S(1)} %get-tuple-element.16), channel_id=1, replica_groups=mesh['zb'=4,'za'=2,'xb'=2,'xa'=2,'x_lo'=2,'y'=8,'core'=2] {'x_lo','y'}, dimensions={0} | all-to-all | bytes 1179648 | tf_op jit(solution)/shard_map/all_to_all | solution.py:188
  108.8 1.9 %collective-permute-start.3 = (bf16[16,144,128]{2,1,0:T(8,128)(2,1)S(1)}, bf16[16,144,128]{2,1,0:T(8,128)(2,1)S(1)}, u32[]{:S(2)}, u32[]{:S(2)}) collective-permute-start(bf16[16,144,128]{2,1,0:T(8,128)(2,1)S(1)} %all_to_all.27.own_ref), channel_id=1, source_target_pairs={{0,1},{1,0},{2,3},{3,2},{4,5},{5,4},{6,7},{7,6},{8,9},{9,8},{10,11... | collective-permute-start | bytes 1769480 | tf_op jit(solution)/shard_map/ppermute | solution.py:189
  110.7 2.0 %collective-permute-done.3.other_ref = bf16[16,144,128]{2,1,0:T(8,128)(2,1)S(1)} collective-permute-done((bf16[16,144,128]{2,1,0:T(8,128)(2,1)S(1)}, bf16[16,144,128]{2,1,0:T(8,128)(2,1)S(1)}, u32[]{:S(2)}, u32[]{:S(2)}) %collective-permute-start.3) | collective-permute-done | bytes 589856 | tf_op jit(solution)/shard_map/ppermute | solution.py:189
  112.7 1.5 backward_tiles.1
  114.2 1.9 %collective-permute-start.4 = (bf16[1040,128]{1,0:T(8,128)(2,1)S(1)}, bf16[1040,128]{1,0:T(8,128)(2,1)S(1)}, u32[]{:S(2)}, u32[]{:S(2)}) collective-permute-start(bf16[1040,128]{1,0:T(8,128)(2,1)S(1)} %get-tuple-element.19), channel_id=1, source_target_pairs={{0,128},{128,256},{256,384},{384,512},{512,640},{640,768},{768,896... | collective-permute-start | bytes 798728 | tf_op jit(solution)/shard_map/ppermute | solution.py:202
  116.1 5.1 %collective-permute-start.5 = (bf16[1024,128]{1,0:T(8,128)(2,1)S(1)}, bf16[1024,128]{1,0:T(8,128)(2,1)S(1)}, u32[]{:S(2)}, u32[]{:S(2)}) collective-permute-start(bf16[1024,128]{1,0:T(8,128)(2,1)S(1)} %get-tuple-element.20), channel_id=1, source_target_pairs={{0,896},{128,0},{256,128},{384,256},{512,384},{640,512},{768,640},... | collective-permute-start | bytes 786440 | tf_op jit(solution)/shard_map/ppermute | solution.py:203
  121.3 5.6 %collective-permute-done.5.high_ref = bf16[1024,128]{1,0:T(8,128)(2,1)S(1)} collective-permute-done((bf16[1024,128]{1,0:T(8,128)(2,1)S(1)}, bf16[1024,128]{1,0:T(8,128)(2,1)S(1)}, u32[]{:S(2)}, u32[]{:S(2)}) %collective-permute-start.5) | collective-permute-done | bytes 262176 | tf_op jit(solution)/shard_map/ppermute | solution.py:203
  126.8 0.0 collective-permute-done.4.low_ref
  126.8 0.1 middle.1
  126.9 30.1 %all_to_all.28.terms_ref = bf16[16,144,128]{2,1,0:T(8,128)(2,1)S(1)} all-to-all(bf16[16,144,128]{2,1,0:T(8,128)(2,1)S(1)} %middle.1), channel_id=1, replica_groups=mesh['zb'=4,'za'=2,'xb'=2,'xa'=2,'x_lo'=2,'y'=8,'core'=2] {'xb','xa','zb'}, dimensions={0} | all-to-all | bytes 1179648 | tf_op jit(solution)/shard_map/all_to_all | solution.py:207
  157.1 0.8 final.1
  157.8 12.6 %all_to_all.29 = f32[16,8,256]{2,1,0:T(8,128)S(1)} all-to-all(f32[16,8,256]{2,1,0:T(8,128)S(1)} %get-tuple-element.22), channel_id=1, replica_groups=mesh['zb'=4,'za'=2,'xb'=2,'xa'=2,'x_lo'=2,'y'=8,'core'=2] {'x_lo','y'}, dimensions={0} | all-to-all | bytes 262144 | tf_op jit(solution)/shard_map/all_to_all | solution.py:214
  170.4 0.7 copy.12
  (1 shorter events, 0.0 us)
Async XLA Ops:
  0.6 56.2 %copy-start.4 = (s32[1,1,48]{2,1,0:T(1,128)S(1)}, s32[1,1,48]{2,1,0:T(1,128)}, u32[]{:S(2)}) copy-start(s32[1,1,48]{2,1,0:T(1,128)} %param.11) | copy-start | bytes 580
  0.6 56.2 %copy-start.3 = (s32[1,1,48]{2,1,0:T(1,128)S(1)}, s32[1,1,48]{2,1,0:T(1,128)}, u32[]{:S(2)}) copy-start(s32[1,1,48]{2,1,0:T(1,128)} %param.10) | copy-start | bytes 580
  0.7 56.2 %copy-start = (bf16[1,1,48,128,128]{4,3,2,1,0:T(8,128)(2,1)S(1)}, bf16[1,1,48,128,128]{4,3,2,1,0:T(8,128)(2,1)}, u32[]{:S(2)}) copy-start(bf16[1,1,48,128,128]{4,3,2,1,0:T(8,128)(2,1)} %param.9) | copy-start | bytes 4718596
  43.5 9.5 %collective-permute-start.1 = (bf16[8,128,128]{2,1,0:T(8,128)(2,1)S(1)}, bf16[8,128,128]{2,1,0:T(8,128)(2,1)S(1)}, u32[]{:S(2)}, u32[]{:S(2)}) collective-permute-start(bf16[8,128,128]{2,1,0:T(8,128)(2,1)S(1)} %get-tuple-element.23), channel_id=1, source_target_pairs={{0,896},{128,0},{256,128},{384,256},{512,384},{640,512},{768,640},... | collective-permute-start | bytes 786440 | tf_op jit(solution)/shard_map/ppermute | solution.py:172
  46.8 10.0 %collective-permute-start = (bf16[8,128,128]{2,1,0:T(8,128)(2,1)S(1)}, bf16[8,128,128]{2,1,0:T(8,128)(2,1)S(1)}, u32[]{:S(2)}, u32[]{:S(2)}) collective-permute-start(bf16[8,128,128]{2,1,0:T(8,128)(2,1)S(1)} %get-tuple-element.24), channel_id=1, source_target_pairs={{0,128},{128,256},{256,384},{384,512},{512,640},{640,768},{768,896... | collective-permute-start | bytes 786440 | tf_op jit(solution)/shard_map/ppermute | solution.py:171
  58.3 3.8 %collective-permute-start.2 = (bf16[16,128,128]{2,1,0:T(8,128)(2,1)S(1)}, bf16[16,128,128]{2,1,0:T(8,128)(2,1)S(1)}, u32[]{:S(2)}, u32[]{:S(2)}) collective-permute-start(bf16[16,128,128]{2,1,0:T(8,128)(2,1)S(1)} %get-tuple-element.14), channel_id=1, source_target_pairs={{0,1},{1,0},{2,3},{3,2},{4,5},{5,4},{6,7},{7,6},{8,9},{9,8},{10,11... | collective-permute-start | bytes 1572872 | tf_op jit(solution)/shard_map/ppermute | solution.py:180
  62.1 23.6 %copy-start.1 = (bf16[128,256]{1,0:T(8,128)(2,1)S(1)}, bf16[128,256]{1,0:T(8,128)(2,1)}, u32[]{:S(2)}) copy-start(bf16[128,256]{1,0:T(8,128)(2,1)} %weight_ref.1) | copy-start | bytes 196612
  62.1 23.6 %copy-start.2 = (bf16[128,256]{1,0:T(8,128)(2,1)S(1)}, bf16[128,256]{1,0:T(8,128)(2,1)}, u32[]{:S(2)}) copy-start(bf16[128,256]{1,0:T(8,128)(2,1)} %cot_ref.1) | copy-start | bytes 196612
  108.8 3.9 %collective-permute-start.3 = (bf16[16,144,128]{2,1,0:T(8,128)(2,1)S(1)}, bf16[16,144,128]{2,1,0:T(8,128)(2,1)S(1)}, u32[]{:S(2)}, u32[]{:S(2)}) collective-permute-start(bf16[16,144,128]{2,1,0:T(8,128)(2,1)S(1)} %all_to_all.27.own_ref), channel_id=1, source_target_pairs={{0,1},{1,0},{2,3},{3,2},{4,5},{5,4},{6,7},{7,6},{8,9},{9,8},{10,11... | collective-permute-start | bytes 1769480 | tf_op jit(solution)/shard_map/ppermute | solution.py:189
  114.2 12.6 %collective-permute-start.4 = (bf16[1040,128]{1,0:T(8,128)(2,1)S(1)}, bf16[1040,128]{1,0:T(8,128)(2,1)S(1)}, u32[]{:S(2)}, u32[]{:S(2)}) collective-permute-start(bf16[1040,128]{1,0:T(8,128)(2,1)S(1)} %get-tuple-element.19), channel_id=1, source_target_pairs={{0,128},{128,256},{256,384},{384,512},{512,640},{640,768},{768,896... | collective-permute-start | bytes 798728 | tf_op jit(solution)/shard_map/ppermute | solution.py:202
  116.1 10.7 %collective-permute-start.5 = (bf16[1024,128]{1,0:T(8,128)(2,1)S(1)}, bf16[1024,128]{1,0:T(8,128)(2,1)S(1)}, u32[]{:S(2)}, u32[]{:S(2)}) collective-permute-start(bf16[1024,128]{1,0:T(8,128)(2,1)S(1)} %get-tuple-element.20), channel_id=1, source_target_pairs={{0,896},{128,0},{256,128},{384,256},{512,384},{640,512},{768,640},... | collective-permute-start | bytes 786440 | tf_op jit(solution)/shard_map/ppermute | solution.py:203

commit v4 on v3

--- a/solution.py
+++ b/solution.py
@@ -90,7 +90,7 @@
 
 
 def backward_kernel(
-    count_ref, rows_ref, cols_ref, tiles_ref, own_ref, other_ref, keep_ref, grad_ref, up_ref, down_ref, acc, stripe
+    count_ref, rows_ref, cols_ref, tiles_ref, own_ref, other_ref, keep_ref, grad_ref, send_ref, acc, stripe
 ):
     core, za = lax.axis_index(CORE), lax.axis_index("za")
     half = own_ref.shape[0]
@@ -110,18 +110,16 @@
     grad_ref[...] = grad
     half = keep_ref.shape[0]
     keep_ref[...] = acc[:half]
-    for i in range(half // 2):
-        up_ref[i * owned : (i + 1) * owned] = acc[half + i].astype(up_ref.dtype)
-        down_ref[i * owned : (i + 1) * owned] = acc[half + half // 2 + i].astype(down_ref.dtype)
-    up_ref[half // 2 * owned :] = grad.astype(up_ref.dtype)
-
-
-def middle_kernel(keep_ref, grad_ref, low_ref, high_ref, out_ref):
+    for i in range(half):
+        send_ref[i * owned : (i + 1) * owned] = acc[half + i].astype(send_ref.dtype)
+    send_ref[half * owned :] = grad.astype(send_ref.dtype)
+
+
+def middle_kernel(keep_ref, grad_ref, came_ref, out_ref):
     half, owned, _ = keep_ref.shape
-    part = half // 2
-    grad = (grad_ref[...] + low_ref[part * owned :].astype(jnp.float32)).astype(out_ref.dtype)
+    grad = (grad_ref[...] + came_ref[half * owned :].astype(jnp.float32)).astype(out_ref.dtype)
     for i in range(half):
-        came = (low_ref if i < part else high_ref)[i % part * owned : (i % part + 1) * owned]
+        came = came_ref[i * owned : (i + 1) * owned]
         out_ref[i, :owned] = (keep_ref[i] + came.astype(jnp.float32)).astype(out_ref.dtype)
         out_ref[i, owned:] = grad
 
@@ -187,22 +185,20 @@
     )(terms, weight, cotangent)
     own = lax.all_to_all(payload, PLANE, 0, 0)
     other = lax.ppermute(own, CORE, swap)
-    keep, grad, to_up, to_down = call(
+    keep, grad, send = call(
         backward_kernel,
         "backward_tiles",
         (
             shape((half, width, owned), f32),
             shape((extra, width), f32),
-            shape((part * width + extra, owned), bf16),
-            shape((part * width, owned), bf16),
+            shape((half * width + extra, owned), bf16),
         ),
         tile_specs,
         [pltpu.VMEM((n_row + 1, width, owned), f32), pltpu.VMEM((2 * n_plane, width, owned), bf16)],
     )(tile_counts, rows, cols, tiles, own, other)
-    low = lax.ppermute(to_up, Z, up)
-    high = lax.ppermute(to_down, Z, down)
-    back = call(middle_kernel, "middle", shape((half, width + extra, owned), bf16), [VMEM_SPEC] * 4)(
-        keep, grad, low, high
+    came = lax.ppermute(send, "za", swap)
+    back = call(middle_kernel, "middle", shape((half, width + extra, owned), bf16), [VMEM_SPEC] * 3)(
+        keep, grad, came
     )
     back = lax.all_to_all(back, GROUP, 0, 0)
     grad_x, piece = call(

time: 172 us -> 175 us (1.017)
  waiting for transfers between devices: 16 us -> 24.4 us
  starting transfers between devices: 16.9 us -> 11.9 us
    ppermute x2 -> x1, waiting for transfers between devices: 5.56 us -> 13.9 us  [shards(): came = lax.ppermute(send, 'za', swap)]
    ppermute x2 -> x1, starting transfers between devices: 7.05 us -> 2.01 us  [shards(): came = lax.ppermute(send, 'za', swap)]
  transfers between devices with their start and end apart: 6 -> 5, of which waited for: 5 -> 5; matrix products, arithmetic and copies ran while one was open for 0% -> 0% of each run, Pallas kernels for 0% -> 0%
where the time goes in v4:
time: 175 us; the launch traced here: 174 us
  blocking collectives  131 us (75%)
  waiting for transfers between devices  24.4 us (14%)
  starting transfers between devices  11.9 us (7%)
  Pallas kernels  4.08 us (2%)
    all_to_all x1, blocking collectives, shards(): own = lax.all_to_all(spread, GROUP, 0, 0)  41.8 us
    all_to_all x1, blocking collectives, shards(): back = lax.all_to_all(back, GROUP, 0, 0)  30.2 us
    all_to_all x1, blocking collectives, shards(): terms = lax.all_to_all(terms, PLANE, 0, 0)  23.4 us
    all_to_all x1, blocking collectives, shards(): own = lax.all_to_all(payload, PLANE, 0, 0)  22.2 us
    ppermute x1, waiting for transfers between devices, shards(): came = lax.ppermute(send, 'za', swap)  13.9 us
    all_to_all x1, blocking collectives, shards(): grad_w = lax.all_to_all(piece, PLANE, 0, 0).reshape(width, hid)  12.9 us
    ppermute x1, waiting for transfers between devices, shards(): low = lax.ppermute(own[:part], Z, up)  3.88 us
  transfers between devices with their start and end apart: 5, of which 5 were waited for; matrix products, arithmetic and copies ran while one was open for 0% of the time, Pallas kernels for 0%

profile of v4, /device:TPU:16, one launch (start us, length us, event | category | flops | bytes accessed | tf_op | source)
XLA Modules:
  0.0 174.2 jit_solution(548529499486976871)
XLA Ops:
  0.6 0.0 copy-start.4
  0.6 0.0 copy-start.3
  0.7 0.0 copy-start
  0.7 1.0 broadcast_in_dim.2
  1.6 41.8 %all_to_all.25.own_ref = bf16[16,128,128]{2,1,0:T(8,128)(2,1)S(1)} all-to-all(bf16[16,128,128]{2,1,0:T(8,128)(2,1)S(1)} %broadcast_in_dim.2), channel_id=1, replica_groups=mesh['zb'=4,'za'=2,'xb'=2,'xa'=2,'x_lo'=2,'y'=8,'core'=2] {'xb','xa','zb'}, dimensions={0} | all-to-all | bytes 1048576 | tf_op jit(solution)/shard_map/all_to_all | solution.py:168
  43.5 3.3 %collective-permute-start.1 = (bf16[8,128,128]{2,1,0:T(8,128)(2,1)S(1)}, bf16[8,128,128]{2,1,0:T(8,128)(2,1)S(1)}, u32[]{:S(2)}, u32[]{:S(2)}) collective-permute-start(bf16[8,128,128]{2,1,0:T(8,128)(2,1)S(1)} %get-tuple-element.21), channel_id=1, source_target_pairs={{0,896},{128,0},{256,128},{384,256},{512,384},{640,512},{768,640},... | collective-permute-start | bytes 786440 | tf_op jit(solution)/shard_map/ppermute | solution.py:170
  46.8 2.7 %collective-permute-start = (bf16[8,128,128]{2,1,0:T(8,128)(2,1)S(1)}, bf16[8,128,128]{2,1,0:T(8,128)(2,1)S(1)}, u32[]{:S(2)}, u32[]{:S(2)}) collective-permute-start(bf16[8,128,128]{2,1,0:T(8,128)(2,1)S(1)} %get-tuple-element.22), channel_id=1, source_target_pairs={{0,128},{128,256},{256,384},{384,512},{512,640},{640,768},{768,896... | collective-permute-start | bytes 786440 | tf_op jit(solution)/shard_map/ppermute | solution.py:169
  50.2 2.8 %collective-permute-done.1.high_ref = bf16[8,128,128]{2,1,0:T(8,128)(2,1)S(1)} collective-permute-done((bf16[8,128,128]{2,1,0:T(8,128)(2,1)S(1)}, bf16[8,128,128]{2,1,0:T(8,128)(2,1)S(1)}, u32[]{:S(2)}, u32[]{:S(2)}) %collective-permute-start.1) | collective-permute-done | bytes 262176 | tf_op jit(solution)/shard_map/ppermute | solution.py:170
  52.9 3.9 %collective-permute-done.low_ref = bf16[8,128,128]{2,1,0:T(8,128)(2,1)S(1)} collective-permute-done((bf16[8,128,128]{2,1,0:T(8,128)(2,1)S(1)}, bf16[8,128,128]{2,1,0:T(8,128)(2,1)S(1)}, u32[]{:S(2)}, u32[]{:S(2)}) %collective-permute-start) | collective-permute-done | bytes 262176 | tf_op jit(solution)/shard_map/ppermute | solution.py:169
  56.8 0.0 copy-done.4
  56.8 0.0 copy-done.3
  56.8 0.0 copy-done
  56.8 1.2 forward_tiles.1
  58.0 1.9 %collective-permute-start.2 = (bf16[16,128,128]{2,1,0:T(8,128)(2,1)S(1)}, bf16[16,128,128]{2,1,0:T(8,128)(2,1)S(1)}, u32[]{:S(2)}, u32[]{:S(2)}) collective-permute-start(bf16[16,128,128]{2,1,0:T(8,128)(2,1)S(1)} %get-tuple-element.13), channel_id=1, source_target_pairs={{0,1},{1,0},{2,3},{3,2},{4,5},{5,4},{6,7},{7,6},{8,9},{9,8},{10,11... | collective-permute-start | bytes 1572872 | tf_op jit(solution)/shard_map/ppermute | solution.py:178
  59.9 1.9 %collective-permute-done.2 = bf16[16,128,128]{2,1,0:T(8,128)(2,1)S(1)} collective-permute-done((bf16[16,128,128]{2,1,0:T(8,128)(2,1)S(1)}, bf16[16,128,128]{2,1,0:T(8,128)(2,1)S(1)}, u32[]{:S(2)}, u32[]{:S(2)}) %collective-permute-start.2) | collective-permute-done | bytes 524320 | tf_op jit(solution)/shard_map/ppermute | solution.py:178
  61.8 0.0 copy-start.1
  61.8 0.0 copy-start.2
  61.8 0.1 add_convert_fusion
  62.0 23.4 %all_to_all.26.terms_ref = bf16[16,128,128]{2,1,0:T(8,128)(2,1)S(1)} all-to-all(bf16[16,128,128]{2,1,0:T(8,128)(2,1)S(1)} %add_convert_fusion), channel_id=1, replica_groups=mesh['zb'=4,'za'=2,'xb'=2,'xa'=2,'x_lo'=2,'y'=8,'core'=2] {'x_lo','y'}, dimensions={0} | all-to-all | bytes 1048576 | tf_op jit(solution)/shard_map/all_to_all | solution.py:179
  85.4 0.0 copy-done.1
  85.4 0.0 copy-done.2
  85.4 0.8 dense.1
  86.2 22.2 %all_to_all.27.own_ref = bf16[16,144,128]{2,1,0:T(8,128)(2,1)S(1)} all-to-all(bf16[16,144,128]{2,1,0:T(8,128)(2,1)S(1)} %get-tuple-element.15), channel_id=1, replica_groups=mesh['zb'=4,'za'=2,'xb'=2,'xa'=2,'x_lo'=2,'y'=8,'core'=2] {'x_lo','y'}, dimensions={0} | all-to-all | bytes 1179648 | tf_op jit(solution)/shard_map/all_to_all | solution.py:186
  108.5 1.9 %collective-permute-start.3 = (bf16[16,144,128]{2,1,0:T(8,128)(2,1)S(1)}, bf16[16,144,128]{2,1,0:T(8,128)(2,1)S(1)}, u32[]{:S(2)}, u32[]{:S(2)}) collective-permute-start(bf16[16,144,128]{2,1,0:T(8,128)(2,1)S(1)} %all_to_all.27.own_ref), channel_id=1, source_target_pairs={{0,1},{1,0},{2,3},{3,2},{4,5},{5,4},{6,7},{7,6},{8,9},{9,8},{10,11... | collective-permute-start | bytes 1769480 | tf_op jit(solution)/shard_map/ppermute | solution.py:187
  110.4 2.0 %collective-permute-done.3.other_ref = bf16[16,144,128]{2,1,0:T(8,128)(2,1)S(1)} collective-permute-done((bf16[16,144,128]{2,1,0:T(8,128)(2,1)S(1)}, bf16[16,144,128]{2,1,0:T(8,128)(2,1)S(1)}, u32[]{:S(2)}, u32[]{:S(2)}) %collective-permute-start.3) | collective-permute-done | bytes 589856 | tf_op jit(solution)/shard_map/ppermute | solution.py:187
  112.4 1.2 backward_tiles.1
  113.6 2.0 %collective-permute-start.4 = (bf16[2064,128]{1,0:T(8,128)(2,1)S(1)}, bf16[2064,128]{1,0:T(8,128)(2,1)S(1)}, u32[]{:S(2)}, u32[]{:S(2)}) collective-permute-start(bf16[2064,128]{1,0:T(8,128)(2,1)S(1)} %get-tuple-element.18), channel_id=1, source_target_pairs={{0,128},{128,0},{1,129},{129,1},{2,130},{130,2},{3,131},{131,3},{4... | collective-permute-start | bytes 1585160 | tf_op jit(solution)/shard_map/ppermute | solution.py:199
  115.6 13.9 %collective-permute-done.4.came_ref = bf16[2064,128]{1,0:T(8,128)(2,1)S(1)} collective-permute-done((bf16[2064,128]{1,0:T(8,128)(2,1)S(1)}, bf16[2064,128]{1,0:T(8,128)(2,1)S(1)}, u32[]{:S(2)}, u32[]{:S(2)}) %collective-permute-start.4) | collective-permute-done | bytes 528416 | tf_op jit(solution)/shard_map/ppermute | solution.py:199
  129.5 0.1 middle.1
  129.6 30.2 %all_to_all.28.terms_ref = bf16[16,144,128]{2,1,0:T(8,128)(2,1)S(1)} all-to-all(bf16[16,144,128]{2,1,0:T(8,128)(2,1)S(1)} %middle.1), channel_id=1, replica_groups=mesh['zb'=4,'za'=2,'xb'=2,'xa'=2,'x_lo'=2,'y'=8,'core'=2] {'xb','xa','zb'}, dimensions={0} | all-to-all | bytes 1179648 | tf_op jit(solution)/shard_map/all_to_all | solution.py:203
  159.8 0.8 final.1
  160.6 12.9 %all_to_all.29 = f32[16,8,256]{2,1,0:T(8,128)S(1)} all-to-all(f32[16,8,256]{2,1,0:T(8,128)S(1)} %get-tuple-element.20), channel_id=1, replica_groups=mesh['zb'=4,'za'=2,'xb'=2,'xa'=2,'x_lo'=2,'y'=8,'core'=2] {'x_lo','y'}, dimensions={0} | all-to-all | bytes 262144 | tf_op jit(solution)/shard_map/all_to_all | solution.py:210
  173.5 0.7 copy.12
  (1 shorter events, 0.0 us)
Async XLA Ops:
  0.6 56.2 %copy-start.4 = (s32[1,1,48]{2,1,0:T(1,128)S(1)}, s32[1,1,48]{2,1,0:T(1,128)}, u32[]{:S(2)}) copy-start(s32[1,1,48]{2,1,0:T(1,128)} %param.11) | copy-start | bytes 580
  0.6 56.2 %copy-start.3 = (s32[1,1,48]{2,1,0:T(1,128)S(1)}, s32[1,1,48]{2,1,0:T(1,128)}, u32[]{:S(2)}) copy-start(s32[1,1,48]{2,1,0:T(1,128)} %param.10) | copy-start | bytes 580
  0.7 56.2 %copy-start = (bf16[1,1,48,128,128]{4,3,2,1,0:T(8,128)(2,1)S(1)}, bf16[1,1,48,128,128]{4,3,2,1,0:T(8,128)(2,1)}, u32[]{:S(2)}) copy-start(bf16[1,1,48,128,128]{4,3,2,1,0:T(8,128)(2,1)} %param.9) | copy-start | bytes 4718596
  43.5 9.5 %collective-permute-start.1 = (bf16[8,128,128]{2,1,0:T(8,128)(2,1)S(1)}, bf16[8,128,128]{2,1,0:T(8,128)(2,1)S(1)}, u32[]{:S(2)}, u32[]{:S(2)}) collective-permute-start(bf16[8,128,128]{2,1,0:T(8,128)(2,1)S(1)} %get-tuple-element.21), channel_id=1, source_target_pairs={{0,896},{128,0},{256,128},{384,256},{512,384},{640,512},{768,640},... | collective-permute-start | bytes 786440 | tf_op jit(solution)/shard_map/ppermute | solution.py:170
  46.8 10.0 %collective-permute-start = (bf16[8,128,128]{2,1,0:T(8,128)(2,1)S(1)}, bf16[8,128,128]{2,1,0:T(8,128)(2,1)S(1)}, u32[]{:S(2)}, u32[]{:S(2)}) collective-permute-start(bf16[8,128,128]{2,1,0:T(8,128)(2,1)S(1)} %get-tuple-element.22), channel_id=1, source_target_pairs={{0,128},{128,256},{256,384},{384,512},{512,640},{640,768},{768,896... | collective-permute-start | bytes 786440 | tf_op jit(solution)/shard_map/ppermute | solution.py:169
  58.0 3.8 %collective-permute-start.2 = (bf16[16,128,128]{2,1,0:T(8,128)(2,1)S(1)}, bf16[16,128,128]{2,1,0:T(8,128)(2,1)S(1)}, u32[]{:S(2)}, u32[]{:S(2)}) collective-permute-start(bf16[16,128,128]{2,1,0:T(8,128)(2,1)S(1)} %get-tuple-element.13), channel_id=1, source_target_pairs={{0,1},{1,0},{2,3},{3,2},{4,5},{5,4},{6,7},{7,6},{8,9},{9,8},{10,11... | collective-permute-start | bytes 1572872 | tf_op jit(solution)/shard_map/ppermute | solution.py:178
  61.8 23.6 %copy-start.1 = (bf16[128,256]{1,0:T(8,128)(2,1)S(1)}, bf16[128,256]{1,0:T(8,128)(2,1)}, u32[]{:S(2)}) copy-start(bf16[128,256]{1,0:T(8,128)(2,1)} %weight_ref.1) | copy-start | bytes 196612
  61.8 23.6 %copy-start.2 = (bf16[128,256]{1,0:T(8,128)(2,1)S(1)}, bf16[128,256]{1,0:T(8,128)(2,1)}, u32[]{:S(2)}) copy-start(bf16[128,256]{1,0:T(8,128)(2,1)} %cot_ref.1) | copy-start | bytes 196612
  108.5 3.9 %collective-permute-start.3 = (bf16[16,144,128]{2,1,0:T(8,128)(2,1)S(1)}, bf16[16,144,128]{2,1,0:T(8,128)(2,1)S(1)}, u32[]{:S(2)}, u32[]{:S(2)}) collective-permute-start(bf16[16,144,128]{2,1,0:T(8,128)(2,1)S(1)} %all_to_all.27.own_ref), channel_id=1, source_target_pairs={{0,1},{1,0},{2,3},{3,2},{4,5},{5,4},{6,7},{7,6},{8,9},{9,8},{10,11... | collective-permute-start | bytes 1769480 | tf_op jit(solution)/shard_map/ppermute | solution.py:187
  113.6 15.9 %collective-permute-start.4 = (bf16[2064,128]{1,0:T(8,128)(2,1)S(1)}, bf16[2064,128]{1,0:T(8,128)(2,1)S(1)}, u32[]{:S(2)}, u32[]{:S(2)}) collective-permute-start(bf16[2064,128]{1,0:T(8,128)(2,1)S(1)} %get-tuple-element.18), channel_id=1, source_target_pairs={{0,128},{128,0},{1,129},{129,1},{2,130},{130,2},{3,131},{131,3},{4... | collective-permute-start | bytes 1585160 | tf_op jit(solution)/shard_map/ppermute | solution.py:199
